TPU v7x, 32 devices: a whole 2x2x4 slice. The times are simulated.
32 devices in a mesh: segment: 4 (over x, core), blk: 8 (over z, y).
Axes of the slice: x: 2, y: 2, z: 4, core: 2. Of those that a mesh axis runs over, the one named last changes fastest.
Arguments:
- fresh: bfloat16 [256, 4096], replicated, may hold values from -6 to 6
- previous: bfloat16 [4, 256, 4096], P('segment'), may hold values from -6 to 6
- span_index: int32 [4], P('segment'), may hold values from 0 to 7
- cache_counts: int32 [4, 8], P('segment'), may hold values from 1 to 2048, 8192 in all within a row
- norm_gain: float32 [4, 4096], P('segment'), may hold values from 0.1 to 1.9
- w_query: bfloat16 [4, 4096, 4096], P('segment', None, 'blk'), may hold values from -0.375 to 0.375
- w_keyval: bfloat16 [4, 4096, 2048], P('segment', None, 'blk'), may hold values from -0.09375 to 0.09375
- w_out: bfloat16 [4, 4096, 4096], P('segment', 'blk'), may hold values from -0.09375 to 0.09375
- cache_keys: bfloat16 [4, 16384, 1024], P('segment', 'blk'), may hold values from -220 to 220
- cache_values: bfloat16 [4, 16384, 1024], P('segment', 'blk'), may hold values from -6 to 6
Outputs:
- mixed: bfloat16 [4, 256, 4096], P('segment')
Inputs may be any that keep to these rules, and one draw needn't show every extreme that they name: Each row of cache_counts sums to 8192 and its largest entry is 2048.
All inputs are finite; a program needn't handle non-finite values.
Results may differ from a plain program's by a relative error of at most 0.012.
Values may be sent and summed in bfloat16 or wider, within the bound.
A program may use at most 128 MiB of HBM per device.

v0:
```python
import jax
import jax.numpy as jnp
from jax import lax
from jax.sharding import PartitionSpec as P

KVH = 8
HD = 128


ROPE_BASE = 500000.0
EPSILON = 1e-05


def passed_along(block, axis, distance):
    devices = range(lax.axis_size(axis))
    route = [(i - distance, i) for i in devices if i - distance in devices]
    return lax.ppermute(block, axis, route)


def swapped(block, axis, distance):
    count = lax.axis_size(axis)
    route = []
    for low in range(count):
        high = low | 1 << distance
        if high != low and high < count:
            route += [(low, high), (high, low)]
    return lax.ppermute(block, axis, route)


def rotate(projected, first_span):
    length = projected.shape[0]
    half_width = projected.shape[-1] // 2
    positions = (first_span * length + jnp.arange(length, dtype=jnp.int32)).astype(jnp.float32)
    inverse = ROPE_BASE ** (
        -(jnp.arange(half_width, dtype=jnp.float32) * 2.0) / projected.shape[-1]
    )
    angles = positions[:, None] * inverse[None, :]
    cosine = jnp.cos(angles)[:, None, :]
    sine_table = jnp.sin(angles)[:, None, :]
    left_part = projected[..., :half_width]
    right_part = projected[..., half_width:]
    return jnp.concatenate(
        [
            left_part * cosine - right_part * sine_table,
            right_part * cosine + left_part * sine_table,
        ],
        axis=-1,
    )


def attend_rows(query_rows, key_rows, value_rows, allowed):
    scores = lax.dot_general(
        query_rows, key_rows, (((1,), (1,)), ((), ())), preferred_element_type=jnp.float32
    ) * query_rows.shape[-1] ** (-0.5)
    scores = jnp.where(allowed, scores, -jnp.inf)
    highest = jnp.max(scores, axis=-1, keepdims=True)
    weights = jnp.exp(scores - highest)
    totals = jnp.sum(weights, axis=-1, keepdims=True)
    partial_out = (
        jnp.dot(weights.astype(jnp.bfloat16), value_rows, preferred_element_type=jnp.float32)
        / totals
    ).astype(jnp.bfloat16)
    return (partial_out, (highest + jnp.log(totals))[:, 0])


def shards(
    fresh,
    previous,
    span_index,
    cache_counts,
    norm_gain,
    w_query,
    w_keyval,
    w_out,
    cache_keys,
    cache_values,
):
    blocks = lax.axis_size("blk")
    position = lax.axis_index("blk")
    span_rows = fresh.shape[0]
    arrived = passed_along(previous[0], "segment", 1)
    current = jnp.where(lax.axis_index("segment") == 0, fresh, arrived)
    widened = current.astype(jnp.float32)
    normed = (
        widened
        * lax.rsqrt(jnp.mean(widened * widened, axis=-1, keepdims=True) + EPSILON)
        * norm_gain[0]
    ).astype(jnp.bfloat16)
    first_span = span_index[0]
    heads_here = w_query.shape[2] // HD
    ratio = blocks // KVH
    queries = jnp.dot(normed, w_query[0], preferred_element_type=jnp.float32).reshape(
        span_rows, heads_here, HD
    )
    queries = rotate(queries, first_span).astype(jnp.bfloat16).reshape(span_rows, heads_here * HD)
    projected = jnp.dot(normed, w_keyval[0], preferred_element_type=jnp.float32)
    if ratio == 2:
        odd_member = position % 2 == 1
        as_key = rotate(projected[:, None, :], first_span)[:, 0, :].astype(jnp.bfloat16)
        mine = jnp.where(odd_member, projected.astype(jnp.bfloat16), as_key)
        partner = swapped(mine, "blk", 0)
        own_keys = jnp.where(odd_member, partner, mine)
        own_values = jnp.where(odd_member, mine, partner)
    else:
        own_keys = rotate(projected[:, None, :HD], first_span)[:, 0, :].astype(jnp.bfloat16)
        own_values = projected[:, HD:].astype(jnp.bfloat16)
    query_rows = queries.reshape(span_rows * heads_here, HD)
    row_tokens = jnp.arange(span_rows * heads_here, dtype=jnp.int32) // heads_here
    causal = row_tokens[:, None] >= jnp.arange(span_rows, dtype=jnp.int32)[None, :]
    own_out, own_log = attend_rows(query_rows, own_keys, own_values, causal)
    own_out = own_out.reshape(span_rows, heads_here * HD)
    own_log = own_log.reshape(span_rows, heads_here).T
    cache_rows = cache_keys.shape[1]
    offsets = jnp.arange(cache_rows, dtype=jnp.int32)
    every_query = lax.all_gather(queries, "blk", axis=0, tiled=True)
    live = cache_counts[0, position]

    def holder(source):
        query_block = lax.dynamic_slice_in_dim(
            every_query, source * span_rows, span_rows, 0
        ).reshape(span_rows * heads_here, HD)
        head_start = source // ratio * HD
        key_rows = lax.dynamic_slice_in_dim(cache_keys[0], head_start, HD, 1)
        value_rows = lax.dynamic_slice_in_dim(cache_values[0], head_start, HD, 1)
        partial_out, log_totals = attend_rows(
            query_block, key_rows, value_rows, (offsets < live)[None, :]
        )
        return (
            partial_out.reshape(span_rows, heads_here * HD),
            log_totals.reshape(span_rows, heads_here).T,
        )

    held_outs, held_logs = lax.map(holder, jnp.arange(blocks, dtype=jnp.int32))
    shard_outs = lax.all_to_all(held_outs, "blk", split_axis=0, concat_axis=0, tiled=True)
    shard_logs = lax.all_to_all(held_logs, "blk", split_axis=0, concat_axis=0, tiled=True)
    all_outs = (
        jnp.concatenate([own_out[None], shard_outs], axis=0)
        .astype(jnp.float32)
        .reshape(blocks + 1, span_rows, heads_here, HD)
    )
    all_logs = jnp.concatenate([own_log[None], shard_logs], axis=0).transpose(0, 2, 1)
    ceiling = jnp.max(all_logs, axis=0)
    factors = jnp.exp(all_logs - ceiling)
    attended = (
        jnp.sum(factors[..., None] * all_outs, axis=0) / jnp.sum(factors, axis=0)[..., None]
    ).astype(jnp.bfloat16)
    attended = attended.reshape(span_rows, heads_here * HD)
    head_terms = lax.optimization_barrier(
        jnp.dot(attended, w_out[0], preferred_element_type=jnp.float32).astype(jnp.bfloat16)
    ).astype(jnp.float32)
    summed = lax.psum(head_terms.astype(jnp.bfloat16), "blk").astype(jnp.float32)
    mixed = (widened + summed).astype(jnp.bfloat16)
    return mixed[None]


def solution(mesh):
    placed = (
        P(),
        P("segment", None, None),
        P("segment"),
        P("segment", None),
        P("segment", None),
        P("segment", None, "blk"),
        P("segment", None, "blk"),
        P("segment", "blk", None),
        P("segment", "blk", None),
        P("segment", "blk", None),
    )
    return jax.shard_map(
        shards, mesh=mesh, in_specs=placed, out_specs=P("segment", None, None), check_vma=False
    )
```

profile of v0, /device:TPU:2, one launch (start us, length us, event | category | flops | bytes accessed | tf_op | source)
XLA Modules:
  0.0 377.0 jit_solution(7249632805387359731)
XLA Ops:
  6.5 2.0 collective-permute-start
  8.6 6.4 %copy.33 = bf16[512,4096]{1,0:T(8,128)(2,1)} copy(bf16[512,4096]{0,1:T(8,128)(2,1)} %bitcast.72) | data formatting | bytes 8388608 | tf_op jit(solution)/shard_map/dot_general | solution.py:92
  16.0 18.3 %collective-permute-done = bf16[256,4096]{1,0:T(8,128)(2,1)} collective-permute-done((bf16[256,4096]{1,0:T(8,128)(2,1)}, bf16[256,4096]{1,0:T(8,128)(2,1)}, u32[]{:S(2)}, u32[]{:S(2)}) %collective-permute-start) | collective-permute-done | bytes 2097184 | tf_op jit(solution)/shard_map/ppermute | solution.py:17
  34.3 2.5 fusion.23
  36.9 1.4 fusion.31
  38.4 0.9 copy.28
  39.9 50.1 %all-gather.2.cloned.1.call-done = bf16[2048,512]{1,0:T(8,128)(2,1)} async-done(((bf16[256,512]{1,0:T(8,128)(2,1)}), bf16[2048,512]{1,0:T(8,128)(2,1)}) %all-gather.2.cloned.1.call-update) | async-done | bytes 2097168 | tf_op jit(solution)/shard_map/all_gather | solution.py:115
  90.0 101.6 %while.15 = (s32[]{:T(128)}, bf16[8,256,512]{2,1,0:T(8,128)(2,1)}, f32[8,4,256]{2,1,0:T(4,128)S(1)}, s32[]{:T(128)}, s32[8]{0:T(128)S(1)}, /*index=5*/bf16[2048,...) while((s32[]{:T(128)}, bf16[8,256,512]{2,1,0:T(8,128)(2,1)}, ...), condition=%wide.region_6.7_spmd.clone, body=%wide.region_3.6_spmd.clone.sunk | while | flops 1097073664 | bytes 28901644 | solution.py:133
  90.6 0.6 dynamic_slice.52
  91.8 1.0 constant_dynamic-slice_fusion.3
  93.6 2.5 fusion.74
  96.0 2.2 fusion.75
  98.2 3.3 fusion.76
  101.7 0.7 constant_dynamic-update-slice_fusion.4
  103.3 0.6 dynamic_slice.52
  104.5 1.0 constant_dynamic-slice_fusion.3
  106.3 2.5 fusion.74
  108.7 2.2 fusion.75
  110.9 3.3 fusion.76
  114.4 0.7 constant_dynamic-update-slice_fusion.4
  116.0 0.6 dynamic_slice.52
  117.2 1.0 constant_dynamic-slice_fusion.3
  119.0 2.5 fusion.74
  121.4 2.2 fusion.75
  123.6 3.3 fusion.76
  127.1 0.7 constant_dynamic-update-slice_fusion.4
  129.9 1.0 constant_dynamic-slice_fusion.3
  131.7 2.5 fusion.74
  134.1 2.2 fusion.75
  136.3 3.3 fusion.76
  139.8 0.7 constant_dynamic-update-slice_fusion.4
  142.6 1.0 constant_dynamic-slice_fusion.3
  144.4 2.5 fusion.74
  146.8 2.2 fusion.75
  149.0 3.3 fusion.76
  152.5 0.7 constant_dynamic-update-slice_fusion.4
  155.3 1.0 constant_dynamic-slice_fusion.3
  157.1 2.5 fusion.74
  159.5 2.2 fusion.75
  161.7 3.3 fusion.76
  165.2 0.7 constant_dynamic-update-slice_fusion.4
  168.0 1.0 constant_dynamic-slice_fusion.3
  169.8 2.5 fusion.74
  172.2 2.2 fusion.75
  174.4 3.3 fusion.76
  177.9 0.7 constant_dynamic-update-slice_fusion.4
  179.5 0.6 dynamic_slice.52
  180.7 1.0 constant_dynamic-slice_fusion.3
  182.5 2.5 fusion.74
  184.9 2.2 fusion.75
  187.1 3.3 fusion.76
  190.6 0.7 constant_dynamic-update-slice_fusion.4
  191.6 9.6 %all_to_all.10 = f32[8,4,256]{2,1,0:T(4,128)S(1)} all-to-all(f32[8,4,256]{2,1,0:T(4,128)S(1)} %get-tuple-element.121), channel_id=1, replica_groups=mesh['segment'=4,'blk'=8] {'blk'}, dimensions={0} | all-to-all | bytes 65536 | tf_op jit(solution)/shard_map/all_to_all | solution.py:135
  201.2 4.3 %all-to-all-start.1 = ((bf16[8,256,512]{2,1,0:T(8,128)(2,1)}), bf16[8,256,512]{2,1,0:T(8,128)(2,1)}, u32[]{:S(2)}, u32[]{:S(2)}) async-start(bf16[8,256,512]{2,1,0:T(8,128)(2,1)} %get-tuple-element.122), calls=%async_computation.1 | async-start | bytes 4194304 | tf_op jit(solution)/shard_map/all_to_all | solution.py:134
  205.7 0.9 copy.27
  206.6 0.9 copy.26
  207.5 2.8 fusion.29
  211.5 2.0 fusion.34
  214.1 38.5 %all-to-all-done.1 = bf16[8,256,512]{2,1,0:T(8,128)(2,1)} async-done(((bf16[8,256,512]{2,1,0:T(8,128)(2,1)}), bf16[8,256,512]{2,1,0:T(8,128)(2,1)}, u32[]{:S(2)}, u32[]{:S(2)}) %all-to-all-start.1) | async-done | bytes 2097184 | tf_op jit(solution)/shard_map/all_to_all | solution.py:134
  252.5 4.0 %concatenate.34 = bf16[8,256,4,128]{3,2,1,0:T(4,128)(2,1)} reshape(bf16[8,256,512]{2,1,0:T(8,128)(2,1)} %all-to-all-done.1) | data formatting | bytes 4194304 | tf_op jit(solution)/shard_map/concatenate | solution.py:137
  256.5 5.3 %multiply_reduce_fusion = f32[256,4,128]{2,1,0:T(4,128)S(1)} fusion(bf16[8,256,4,128]{3,2,1,0:T(4,128)(2,1)} %concatenate.34, bf16[1,256,4,128]{3,2,1,0:T(4,128)(2,1)} %bitcast.76, f32[9,256,4]{2,1,0:T(8,128)S(1)} %copy.31), kind=kLoop, calls=%fused_computation.28 | loop fusion | flops 4587520 | bytes 2920448 | tf_op jit(solution)/shard_map/reduce_sum | solution.py:145
  262.2 2.6 convolution_convert_fusion
  264.8 101.0 %all-reduce.2.cloned.1.call-done = bf16[256,4096]{1,0:T(8,128)(2,1)} async-done(((bf16[256,4096]{1,0:T(8,128)(2,1)}), bf16[256,4096]{1,0:T(8,128)(2,1)}) %all-reduce.2.cloned.1.call-update) | async-done | bytes 2097168 | tf_op jit(solution)/shard_map/psum | solution.py:151
  365.8 4.3 %fusion.28 = bf16[1,256,4096]{2,1,0:T(8,128)(2,1)} fusion(bf16[256,4096]{1,0:T(8,128)(2,1)} %all-reduce.2.cloned.1.call-done, bf16[256,4096]{1,0:T(8,128)(2,1)} %copy-done.1), kind=kLoop, calls=%fused_computation.34 | loop fusion | flops 4194304 | bytes 6291456 | tf_op jit(solution)/shard_map/broadcast_in_dim | solution.py:153
  (105 shorter events, 14.8 us)
Async XLA Ops:
  6.5 200.9 %copy-start = (bf16[1,4096,256]{2,1,0:T(8,128)(2,1)S(1)}, bf16[1,4096,256]{2,1,0:T(8,128)(2,1)}, u32[]{:S(2)}) copy-start(bf16[1,4096,256]{2,1,0:T(8,128)(2,1)} %param.18) | copy-start | bytes 6291460
  6.5 83.5 %all-gather.2.cloned.1.call-start = ((), (), s32[]{:S(2)}) async-start(), calls=%async_computation.2 | async-start | bytes 2359296 | tf_op jit(solution)/shard_map/all_gather | solution.py:115
  6.5 27.8 %collective-permute-start = (bf16[256,4096]{1,0:T(8,128)(2,1)}, bf16[256,4096]{1,0:T(8,128)(2,1)}, u32[]{:S(2)}, u32[]{:S(2)}) collective-permute-start(bf16[256,4096]{1,0:T(8,128)(2,1)} %bitcast.80), channel_id=1, source_target_pairs={{0,8},{8,16},{16,24},{1,9},{9,17},{17,25},{2,10},{10,18},{18,26},{... | collective-permute-start | bytes 6291464 | tf_op jit(solution)/shard_map/ppermute | solution.py:17
  15.0 21.9 %copy-start.7 = (f32[1,4096]{1,0:T(1,128)S(1)}, f32[1,4096]{1,0:T(1,128)}, u32[]{:S(2)}) copy-start(f32[1,4096]{1,0:T(1,128)} %param.16) | copy-start | bytes 49156
  15.7 21.2 %copy-start.2 = (bf16[512,4096]{1,0:T(8,128)(2,1)S(1)}, bf16[512,4096]{1,0:T(8,128)(2,1)}, u32[]{:S(2)}) copy-start(bf16[512,4096]{1,0:T(8,128)(2,1)} %copy.33) | copy-start | bytes 12582916
  36.9 1.4 copy-start.1
  36.9 2.4 copy-start.8
  201.2 51.4 %all-to-all-start.1 = ((bf16[8,256,512]{2,1,0:T(8,128)(2,1)}), bf16[8,256,512]{2,1,0:T(8,128)(2,1)}, u32[]{:S(2)}, u32[]{:S(2)}) async-start(bf16[8,256,512]{2,1,0:T(8,128)(2,1)} %get-tuple-element.122), calls=%async_computation.1 | async-start | bytes 4194304 | tf_op jit(solution)/shard_map/all_to_all | solution.py:134
  205.5 160.3 %all-reduce.2.cloned.1.call-start = ((), (), s32[]{:S(2)}) async-start(), calls=%async_computation.3 | async-start | bytes 4194304 | tf_op jit(solution)/shard_map/psum | solution.py:151
  207.5 3.1 copy-start.3
  207.5 3.1 copy-start.4
  210.3 1.0 copy-start.5
  256.5 5.7 %copy-start.6 = (bf16[1,512,4096]{2,1,0:T(8,128)(2,1)S(1)}, bf16[1,512,4096]{2,1,0:T(8,128)(2,1)}, u32[]{:S(2)}) copy-start(bf16[1,512,4096]{2,1,0:T(8,128)(2,1)} %param.19) | copy-start | bytes 12582916
Sparse Core Ops, SparseCore 0:
  39.4 50.5 all-gather.1
  264.9 100.8 all-reduce.1
where the time goes:
time: 380 us; the launch traced here: 377 us
  waiting for transfers between devices  208 us (55%)
  matrix products  55.2 us (15%)
  local copies, waits for them, and re-layouts  37.1 us (10%)
  other arithmetic  35.9 us (9%)
  between operations  14.3 us (4%)
  loops' own time  10.3 us (3%)
  blocking collectives  9.57 us (3%)
  starting transfers between devices  6.61 us (2%)
    psum x1, waiting for transfers between devices, shards(): lax.psum(head_terms.astype(jnp.bfloat16), 'blk').astype(jnp.float32)  101 us
    all_gather x1, waiting for transfers between devices, shards(): every_query = lax.all_gather(queries, 'blk', axis=0, tiled=True)  50.1 us
    all_to_all x1, waiting for transfers between devices, shards(): lax.all_to_all(held_outs, 'blk', split_axis=0, concat_axis=0, tiled=True)  38.5 us
    dot_general x9, matrix products, attend_rows(): jnp.dot(weights.astype(jnp.bfloat16), value_rows, preferred_element_type=...  28.4 us
    dot_general x9, matrix products, attend_rows(): lax.dot_general(query_rows, key_rows, (((1,), (1,)), ((), ())), preferred...  20.1 us
    ppermute x1, waiting for transfers between devices, passed_along(): return lax.ppermute(block, axis, route)  18.3 us
    reduce_sum x9, other arithmetic, attend_rows(): totals = jnp.sum(weights, axis=-1, keepdims=True)  17.9 us
    another operation x1, loops' own time, shards(): held_outs, held_logs = lax.map(holder, jnp.arange(blocks, dtype=jnp.int32))  10.3 us
  transfers between devices with their start and end apart: 4, of which 4 were waited for; matrix products, arithmetic and copies ran while one was open for 4% of the time, Pallas kernels for 0%

commit v1 on v0

--- a/solution.py
+++ b/solution.py
@@ -1,6 +1,10 @@
+import math
+
 import jax
 import jax.numpy as jnp
 from jax import lax
+from jax.experimental import pallas as pl
+from jax.experimental.pallas import tpu as pltpu
 from jax.sharding import PartitionSpec as P
 
 KVH = 8
@@ -153,6 +157,387 @@
     return mixed[None]
 
 
+ROWS = 4
+MESH = pl.DeviceIdType.MESH
+
+
+def near_first(z, step):
+    half = z // 2
+    if isinstance(step, int):
+        return (z, z + 1 - 2 * (z % 2), 2 - half, 3 - 3 * half)[step]
+    pair = z + 1 - 2 * (z % 2)
+    later = jnp.where(step == 2, 2 - half, 3 - 3 * half)
+    return jnp.where(step == 0, z, jnp.where(step == 1, pair, later))
+
+
+def head_columns(rows):
+    return jnp.concatenate([rows] * 16, axis=0).T
+
+
+def head_rows(columns):
+    return columns.T[:8]
+
+
+def plane_kernel(
+    q_ref, ok_ref, ov_ref, bias_ref, cur_hbm, kc_hbm, vc_hbm, wo_hbm, out_ref,
+    qall, kbuf, vbuf, wo, cur, o_keep, l_keep, oy_tx, ly_tx, oy_rx, ly_rx,
+    oz_tx, lz_tx, oz_rx, lz_rx, att, hk, hy_tx, hy_rx, hz_tx, hz_rx,
+    load_sem, q_up, q_down, q_side, q_in, oy_out, oy_in, ly_out, ly_in,
+    oz_out, oz_in, lz_out, lz_in, hy_out, hy_in, hz_out, hz_in,
+    r_up, r_down, r_side, r_in,
+):
+    me = lax.axis_index("blk")
+    z, y = me // 2, me % 2
+    other = z * 2 + 1 - y
+    width = q_ref.shape[1]
+    heads = width // HD
+    tokens = q_ref.shape[0]
+    scale = HD ** (-0.5)
+    to_exp2 = scale * math.log2(math.e)
+
+    def own_cols(c):
+        return pl.ds(pl.multiple_of(c * width, width), width)
+
+    loads = [
+        pltpu.make_async_copy(kc_hbm, kbuf, load_sem.at[0]),
+        pltpu.make_async_copy(vc_hbm, vbuf, load_sem.at[1]),
+        pltpu.make_async_copy(wo_hbm, wo, load_sem.at[2]),
+        pltpu.make_async_copy(cur_hbm.at[:, own_cols(me)], cur, load_sem.at[3]),
+    ]
+    for load in loads:
+        load.start()
+
+    barrier = pltpu.get_barrier_semaphore()
+    pl.semaphore_signal(barrier, inc=1, device_id={"blk": other}, device_id_type=MESH)
+    for step in range(1, ROWS):
+        pl.semaphore_signal(
+            barrier, inc=1, device_id={"blk": near_first(z, step) * 2 + y}, device_id_type=MESH
+        )
+    pl.semaphore_wait(barrier, ROWS)
+
+    def remote(src, dst, out_sem, in_sem, device):
+        return pltpu.make_async_remote_copy(
+            src_ref=src, dst_ref=dst, send_sem=out_sem, recv_sem=in_sem,
+            device_id={"blk": device}, device_id_type=MESH,
+        )
+
+    def spread(view, up, down, side, arrived, row, act):
+        part = view(row * 2 + y)
+        in_sem = arrived.at[row * 2 + y]
+
+        @pl.when(jnp.logical_and(row <= z, z < ROWS - 1))
+        def _():
+            act(remote(part, part, up.at[row], in_sem, me + 2))
+
+        @pl.when(jnp.logical_and(row >= z, z > 0))
+        def _():
+            act(remote(part, part, down.at[row], in_sem, me - 2))
+
+        act(remote(part, part, side.at[row], in_sem, other))
+
+    def start(copy):
+        copy.start()
+
+    def finish(copy):
+        copy.wait_send()
+
+    def q_view(c):
+        return qall.at[c]
+
+    def out_view(c):
+        return out_ref.at[:, own_cols(c)]
+
+    def q_spread(row, act):
+        spread(q_view, q_up, q_down, q_side, q_in, row, act)
+
+    def out_spread(row, act):
+        spread(out_view, r_up, r_down, r_side, r_in, row, act)
+
+    lanes = lax.broadcasted_iota(jnp.int32, (tokens, HD), 1)
+
+    def one_head(q_part, k_part, v_part, bias):
+        scores = lax.dot_general(
+            q_part, k_part, (((1,), (1,)), ((), ())), preferred_element_type=jnp.float32
+        ) + bias
+        highest = jnp.max(scores, axis=-1, keepdims=True)
+        weights = jnp.exp2((scores - highest) * to_exp2)
+        totals = jnp.sum(weights, axis=-1, keepdims=True)
+        partial = jnp.dot(
+            weights.astype(jnp.bfloat16), v_part, preferred_element_type=jnp.float32
+        ) / totals
+        return partial.astype(jnp.bfloat16), highest * scale + jnp.log(totals)
+
+    def y_copies(row):
+        return (
+            remote(oy_tx.at[row], oy_rx.at[row], oy_out.at[row], oy_in.at[row], other),
+            remote(ly_tx.at[row], ly_rx.at[row], ly_out.at[row], ly_in.at[row], other),
+        )
+
+    def z_copies(row):
+        peer = row * 2 + y
+        return (
+            remote(oz_tx.at[row], oz_rx.at[z], oz_out.at[row], oz_in.at[z], peer),
+            remote(lz_tx.at[row], lz_rx.at[z], lz_out.at[row], lz_in.at[z], peer),
+        )
+
+    def merge(row, away):
+        for copy in y_copies(row):
+            copy.wait_recv()
+        l_a, l_b = l_keep[row], head_columns(ly_rx[row])
+        top = jnp.maximum(l_a, l_b)
+        f_a, f_b = jnp.exp(l_a - top), jnp.exp(l_b - top)
+        total = f_a + f_b
+        f_a, f_b = f_a / total, f_b / total
+        o_dst, l_dst, at = (oz_tx, lz_tx, row) if away else (oz_rx, lz_rx, z)
+        l_dst[at] = head_rows(top + jnp.log(total))
+        for h in range(heads):
+            cols = slice(h * HD, (h + 1) * HD)
+            o_dst[at, :, cols] = (
+                f_a[:, h : h + 1] * o_keep[row, :, cols].astype(jnp.float32)
+                + f_b[:, h : h + 1] * oy_rx[row, :, cols].astype(jnp.float32)
+            ).astype(jnp.bfloat16)
+        if away:
+            for copy in z_copies(row):
+                copy.start()
+
+    qall[me] = q_ref[...]
+
+    def visit(t, carry):
+        j, second = t // 2, t % 2
+        row = near_first(z, j)
+        c = row * 2 + jnp.where(second == 0, y, 1 - y)
+
+        @pl.when(t > 0)
+        def _():
+            remote(q_view(c), q_view(c), q_side.at[row], q_in.at[c], other).wait_recv()
+
+        @pl.when(second == 0)
+        def _():
+            q_spread(row, start)
+
+        @pl.when(t == 0)
+        def _():
+            loads[0].wait()
+            loads[1].wait()
+
+        group = pl.ds(pl.multiple_of(c * HD, HD), HD)
+        logs = jnp.zeros((tokens, HD), jnp.float32)
+        for h in range(heads):
+            cols = slice(h * HD, (h + 1) * HD)
+            partial, log_total = one_head(
+                qall[c, :, cols], kbuf[:, group], vbuf[:, group], bias_ref[...]
+            )
+            logs = jnp.where(lanes == h, log_total, logs)
+
+            @pl.when(second == 0)
+            def _():
+                o_keep[row, :, cols] = partial
+
+            @pl.when(second == 1)
+            def _():
+                oy_tx[row, :, cols] = partial
+
+        @pl.when(second == 0)
+        def _():
+            l_keep[row] = logs
+
+        @pl.when(second == 1)
+        def _():
+            ly_tx[row] = head_rows(logs)
+            for copy in y_copies(row):
+                copy.start()
+
+        @pl.when(t == 3)
+        def _():
+            merge(near_first(z, 0), False)
+
+        @pl.when(t == 5)
+        def _():
+            merge(near_first(z, 1), True)
+
+        @pl.when(t == 7)
+        def _():
+            merge(near_first(z, 2), True)
+
+        return carry
+
+    lax.fori_loop(0, 2 * ROWS, visit, 0)
+
+    row_no = lax.broadcasted_iota(jnp.int32, (tokens, tokens), 0)
+    col_no = lax.broadcasted_iota(jnp.int32, (tokens, tokens), 1)
+    causal = jnp.where(row_no >= col_no, 0.0, -jnp.inf)
+    own = []
+    own_logs = jnp.zeros((tokens, HD), jnp.float32)
+    for h in range(heads):
+        partial, log_total = one_head(
+            q_ref[:, h * HD : (h + 1) * HD], ok_ref[...], ov_ref[...], causal
+        )
+        own_logs = jnp.where(lanes == h, log_total, own_logs)
+        own.append(partial)
+
+    merge(near_first(z, 3), True)
+
+    def from_row(row):
+        return (
+            remote(oz_tx.at[row], oz_rx.at[row], oz_out.at[row], oz_in.at[row], row * 2 + y),
+            remote(lz_tx.at[row], lz_rx.at[row], lz_out.at[row], lz_in.at[row], row * 2 + y),
+        )
+
+    for step in range(1, ROWS):
+        for copy in from_row(near_first(z, step)):
+            copy.wait_recv()
+    all_logs = [own_logs] + [head_columns(lz_rx[row]) for row in range(ROWS)]
+    top = all_logs[0]
+    for logs in all_logs[1:]:
+        top = jnp.maximum(top, logs)
+    factors = [jnp.exp(logs - top) for logs in all_logs]
+    total = factors[0]
+    for factor in factors[1:]:
+        total = total + factor
+    factors = [factor / total for factor in factors]
+    for h in range(heads):
+        cols = slice(h * HD, (h + 1) * HD)
+        summed = factors[0][:, h : h + 1] * own[h].astype(jnp.float32)
+        for row in range(ROWS):
+            summed = summed + factors[row + 1][:, h : h + 1] * oz_rx[row, :, cols].astype(
+                jnp.float32
+            )
+        att[:, cols] = summed.astype(jnp.bfloat16)
+
+    def term(c):
+        return jnp.dot(att[...], wo[:, own_cols(c)], preferred_element_type=jnp.float32)
+
+    def side_terms(row):
+        return remote(hy_tx.at[row], hy_rx.at[row], hy_out.at[row], hy_in.at[row], other)
+
+    def row_terms(row, slot):
+        return remote(hz_tx.at[row], hz_rx.at[slot], hz_out.at[row], hz_in.at[slot], row * 2 + y)
+
+    loads[2].wait()
+    loads[3].wait()
+
+    def send_side(i, carry):
+        row = near_first(z, ROWS - 1 - i)
+        hy_tx[row] = term(row * 2 + 1 - y).astype(jnp.bfloat16)
+        side_terms(row).start()
+        return carry
+
+    def keep_own(i, carry):
+        row = near_first(z, ROWS - 1 - i)
+        hk[row] = term(row * 2 + y)
+        return carry
+
+    lax.fori_loop(0, ROWS, send_side, 0)
+    lax.fori_loop(0, ROWS, keep_own, 0)
+    for step in range(ROWS - 1, 0, -1):
+        row = near_first(z, step)
+        side_terms(row).wait_recv()
+        hz_tx[row] = (hk[row] + hy_rx[row].astype(jnp.float32)).astype(jnp.bfloat16)
+        row_terms(row, z).start()
+    side_terms(z).wait_recv()
+    summed = cur[...].astype(jnp.float32) + hk[z] + hy_rx[z].astype(jnp.float32)
+    for step in range(1, ROWS):
+        row = near_first(z, step)
+        row_terms(row, row).wait_recv()
+        summed = summed + hz_rx[row].astype(jnp.float32)
+    out_ref[:, own_cols(me)] = summed.astype(jnp.bfloat16)
+
+    out_spread(z, start)
+    for step in range(1, ROWS):
+        row = near_first(z, step)
+        c = row * 2 + y
+        remote(out_view(c), out_view(c), r_side.at[row], r_in.at[c], other).wait_recv()
+        out_spread(row, start)
+    for row in range(ROWS):
+        c = row * 2 + 1 - y
+        remote(out_view(c), out_view(c), r_side.at[row], r_in.at[c], other).wait_recv()
+
+    for row in range(ROWS):
+        q_spread(row, finish)
+        out_spread(row, finish)
+        side_terms(row).wait_send()
+        for copy in y_copies(row):
+            copy.wait_send()
+    for step in range(1, ROWS):
+        row = near_first(z, step)
+        for copy in z_copies(row):
+            copy.wait_send()
+        row_terms(row, z).wait_send()
+
+
+def plane_call(queries, own_keys, own_values, bias, current, keys, values, w_out):
+    tokens, width = queries.shape
+    slots = keys.shape[0]
+    chunk = (tokens, width)
+    few = (ROWS, 8, tokens)
+    bf16, f32 = jnp.bfloat16, jnp.float32
+    vmem = pl.BlockSpec(memory_space=pltpu.VMEM)
+    anywhere = pl.BlockSpec(memory_space=pl.ANY)
+    rows_of = lambda kind: pltpu.VMEM((ROWS,) + chunk, kind)
+    sems = lambda count: pltpu.SemaphoreType.DMA((count,))
+    logs = pltpu.VMEM(few, f32)
+    return pl.pallas_call(
+        plane_kernel,
+        out_shape=jax.ShapeDtypeStruct(current.shape, bf16),
+        in_specs=[vmem] * 4 + [anywhere] * 4,
+        out_specs=vmem,
+        scratch_shapes=[
+            pltpu.VMEM((2 * ROWS,) + chunk, bf16),
+            pltpu.VMEM(keys.shape, bf16),
+            pltpu.VMEM(values.shape, bf16),
+            pltpu.VMEM(w_out.shape, bf16),
+            pltpu.VMEM(chunk, bf16),
+            rows_of(bf16), pltpu.VMEM((ROWS, tokens, HD), f32),
+            rows_of(bf16), logs, rows_of(bf16), logs,
+            rows_of(bf16), logs, rows_of(bf16), logs,
+            pltpu.VMEM(chunk, bf16),
+            rows_of(f32), rows_of(bf16), rows_of(bf16), rows_of(bf16), rows_of(bf16),
+            sems(4),
+            sems(ROWS), sems(ROWS), sems(ROWS), sems(2 * ROWS),
+        ] + [sems(ROWS)] * 12 + [
+            sems(ROWS), sems(ROWS), sems(ROWS), sems(2 * ROWS),
+        ],
+        compiler_params=pltpu.CompilerParams(
+            collective_id=0, has_side_effects=True, vmem_limit_bytes=56 * 1024 * 1024
+        ),
+        cost_estimate=pl.CostEstimate(
+            flops=4 * tokens * width * slots * 8, bytes_accessed=16 << 20,
+            transcendentals=tokens * slots * 32,
+        ),
+    )(queries, own_keys, own_values, bias, current, keys, values, w_out)
+
+
+def plane_shards(
+    fresh, previous, span_index, cache_counts, norm_gain,
+    w_query, w_keyval, w_out, cache_keys, cache_values,
+):
+    position = lax.axis_index("blk")
+    span_rows = fresh.shape[0]
+    arrived = passed_along(previous[0], "segment", 1)
+    current = jnp.where(lax.axis_index("segment") == 0, fresh, arrived)
+    widened = current.astype(jnp.float32)
+    normed = (
+        widened
+        * lax.rsqrt(jnp.mean(widened * widened, axis=-1, keepdims=True) + EPSILON)
+        * norm_gain[0]
+    ).astype(jnp.bfloat16)
+    first_span = span_index[0]
+    width = w_query.shape[2]
+    queries = jnp.dot(normed, w_query[0], preferred_element_type=jnp.float32)
+    queries = rotate(queries.reshape(span_rows, width // HD, HD), first_span)
+    queries = queries.astype(jnp.bfloat16).reshape(span_rows, width)
+    projected = jnp.dot(normed, w_keyval[0], preferred_element_type=jnp.float32)
+    own_keys = rotate(projected[:, None, :HD], first_span)[:, 0, :].astype(jnp.bfloat16)
+    own_values = projected[:, HD:].astype(jnp.bfloat16)
+    offsets = jnp.arange(cache_keys.shape[1], dtype=jnp.int32)
+    bias = jnp.where(offsets < cache_counts[0, position], 0.0, -jnp.inf)[None, :]
+    mixed = plane_call(
+        queries, own_keys, own_values, bias, current,
+        cache_keys[0], cache_values[0], w_out[0],
+    )
+    return mixed[None]
+
+
 def solution(mesh):
     placed = (
         P(),
@@ -166,6 +551,7 @@
         P("segment", "blk", None),
         P("segment", "blk", None),
     )
+    body = plane_shards if mesh.shape["blk"] == KVH else shards
     return jax.shard_map(
-        shards, mesh=mesh, in_specs=placed, out_specs=P("segment", None, None), check_vma=False
-    )
+        body, mesh=mesh, in_specs=placed, out_specs=P("segment", None, None), check_vma=False
+    )

time: 380 us -> 172 us (0.45)
  the two profiles are of different devices: /device:TPU:2 before, /device:TPU:1 now
where the time goes in v1:
time: 172 us
  Pallas kernels  132 us (77%)
  waiting for transfers between devices  14 us (8%)
  local copies, waits for them, and re-layouts  13.2 us (8%)
  other arithmetic  5.48 us (3%)
  starting transfers between devices  4.63 us (3%)
  matrix products  2.14 us (1%)
    pallas_call x1, Pallas kernels, plane_call(): pl.pallas_call(plane_kernel, out_shape=jax.ShapeDtypeStruct(current.shape...  132 us
    ppermute x1, waiting for transfers between devices, passed_along(): return lax.ppermute(block, axis, route)  14 us
    dot_general x1, local copies, waits for them, and re-layouts, plane_shards(): queries = jnp.dot(normed, w_query[0], preferred_element_type=jnp.float32)  6.43 us
    unnamed x11, local copies, waits for them, and re-layouts  4.67 us
    ppermute x1, starting transfers between devices, passed_along(): return lax.ppermute(block, axis, route)  4.63 us
  transfers between devices with their start and end apart: 1, of which 1 were waited for; matrix products, arithmetic and copies ran while one was open for 5% of the time, Pallas kernels for 0%

profile of v1, /device:TPU:1, one launch (start us, length us, event | category | flops | bytes accessed | tf_op | source)
XLA Modules:
  0.0 171.7 jit_solution(17214035794746104426)
XLA Ops:
  0.0 0.0 copy-start
  0.0 4.6 %collective-permute-start = (bf16[256,4096]{1,0:T(8,128)(2,1)}, bf16[256,4096]{1,0:T(8,128)(2,1)}, u32[]{:S(2)}, u32[]{:S(2)}) collective-permute-start(bf16[256,4096]{1,0:T(8,128)(2,1)} %bitcast.31), channel_id=1, source_target_pairs={{0,8},{8,16},{16,24},{1,9},{9,17},{17,25},{2,10},{10,18},{18,26},{... | collective-permute-start | bytes 6291464 | tf_op jit(solution)/shard_map/ppermute | solution.py:21
  4.6 0.0 copy-start.4
  4.7 6.4 %copy.21 = bf16[512,4096]{1,0:T(8,128)(2,1)} copy(bf16[512,4096]{0,1:T(8,128)(2,1)} %bitcast.24) | data formatting | bytes 8388608 | tf_op jit(solution)/shard_map/dot_general | solution.py:526
  11.7 0.0 copy-done.4
  11.8 0.6 constant_dynamic-slice_fusion
  12.4 1.2 compare_select_fusion.bias_ref
  13.6 0.3 multiply_cosine_fusion.1
  13.9 0.0 copy-start.3
  13.9 14.0 %collective-permute-done = bf16[256,4096]{1,0:T(8,128)(2,1)} collective-permute-done((bf16[256,4096]{1,0:T(8,128)(2,1)}, bf16[256,4096]{1,0:T(8,128)(2,1)}, u32[]{:S(2)}, u32[]{:S(2)}) %collective-permute-start) | collective-permute-done | bytes 2097184 | tf_op jit(solution)/shard_map/ppermute | solution.py:21
  27.9 2.5 %fusion = (f32[256]{0:T(256)S(1)}, bf16[256,4096]{1,0:T(8,128)(2,1)S(1)}) fusion(bf16[256,4096]{1,0:T(8,128)(2,1)} %param.10, bf16[256,4096]{1,0:T(8,128)(2,1)} %collective-permute-done, pred[]{:T(512)S(6)} %eq.3), kind=kLoop, calls=%fused_computation.2 | loop fusion | flops 4194048 | bytes 6292481 | tf_op jit(solution)/shard_map/reduce_sum | solution.py:521
  30.5 0.0 copy-start.2
  30.5 0.0 copy-done
  30.5 0.0 copy-done.3
  30.5 0.0 copy-start.1
  30.5 0.8 fusion.3
  31.3 0.6 slice.41.ov_ref
  31.9 0.0 copy-done.2
  31.9 1.5 copy-done.1
  33.5 1.4 fusion.5
  34.8 0.1 subtract_convert_fusion
  35.0 0.8 copy.22.q_ref
  35.8 0.6 fusion.14
  36.4 0.7 maximum_bitcast_fusion.ok_ref
  37.1 131.5 %shard_map.100 = bf16[256,4096]{1,0:T(8,128)(2,1)} custom-call(bf16[256,512]{1,0:T(8,128)(2,1)} %copy.22.q_ref, bf16[256,128]{1,0:T(8,128)(2,1)} %maximum_bitcast_fusion.ok_ref, bf16[256,128]{1,0:T(8,128)(2,1)} %slice.41.ov_ref, f32[1,2048]{1,0:T(1,128)} %compare_select_fusion.bias_ref, bf16[256,4096]{1,0:T(8,128)(2,1)} %copy-done.2, ...), custom_call_target="tpu_custom_call" | custom-call | flops 8589934592 | bytes 16777216 | tf_op jit(solution)/shard_map/pallas_call | solution.py:479
  168.6 3.1 %copy.25 = bf16[1,256,4096]{2,1,0:T(8,128)(2,1)} copy(bf16[1,256,4096]{2,1,0:T(8,128)(2,1)} %bitcast.26) | data formatting | bytes 4194304
  (5 shorter events, 0.1 us)
Async XLA Ops:
  0.0 30.5 %copy-start = (bf16[1,4096,256]{2,1,0:T(8,128)(2,1)S(1)}, bf16[1,4096,256]{2,1,0:T(8,128)(2,1)}, u32[]{:S(2)}) copy-start(bf16[1,4096,256]{2,1,0:T(8,128)(2,1)} %param.16) | copy-start | bytes 6291460
  0.0 27.9 %collective-permute-start = (bf16[256,4096]{1,0:T(8,128)(2,1)}, bf16[256,4096]{1,0:T(8,128)(2,1)}, u32[]{:S(2)}, u32[]{:S(2)}) collective-permute-start(bf16[256,4096]{1,0:T(8,128)(2,1)} %bitcast.31), channel_id=1, source_target_pairs={{0,8},{8,16},{16,24},{1,9},{9,17},{17,25},{2,10},{10,18},{18,26},{... | collective-permute-start | bytes 6291464 | tf_op jit(solution)/shard_map/ppermute | solution.py:21
  4.6 7.1 %copy-start.4 = (s32[1,8]{1,0:T(1,128)S(1)}, s32[1,8]{1,0:T(1,128)}, u32[]{:S(2)}) copy-start(s32[1,8]{1,0:T(1,128)} %param.13) | copy-start | bytes 100
  13.9 16.6 %copy-start.3 = (f32[1,4096]{1,0:T(1,128)S(1)}, f32[1,4096]{1,0:T(1,128)}, u32[]{:S(2)}) copy-start(f32[1,4096]{1,0:T(1,128)} %param.14) | copy-start | bytes 49156
  30.5 1.5 copy-start.2
  30.5 2.9 %copy-start.1 = (bf16[512,4096]{1,0:T(8,128)(2,1)S(1)}, bf16[512,4096]{1,0:T(8,128)(2,1)}, u32[]{:S(2)}) copy-start(bf16[512,4096]{1,0:T(8,128)(2,1)} %copy.21) | copy-start | bytes 12582916

commit v2 on v1

--- a/solution.py
+++ b/solution.py
@@ -158,6 +158,7 @@
 
 
 ROWS = 4
+PIECES = 8
 MESH = pl.DeviceIdType.MESH
 
 
@@ -170,50 +171,68 @@
     return jnp.where(step == 0, z, jnp.where(step == 1, pair, later))
 
 
-def head_columns(rows):
-    return jnp.concatenate([rows] * 16, axis=0).T
-
-
-def head_rows(columns):
-    return columns.T[:8]
-
-
 def plane_kernel(
-    q_ref, ok_ref, ov_ref, bias_ref, cur_hbm, kc_hbm, vc_hbm, wo_hbm, out_ref,
-    qall, kbuf, vbuf, wo, cur, o_keep, l_keep, oy_tx, ly_tx, oy_rx, ly_rx,
+    counts_ref, gain_ref, cos_ref, sin_ref, fresh_hbm, prev_hbm, wq_hbm, wkv_hbm,
+    kc_hbm, vc_hbm, wo_hbm, out_ref,
+    cur, normed, wq, wkv, own_k, own_v, bias,
+    qall, kbuf, vbuf, wo, parts, logs, oy_rx, ly_rx,
     oz_tx, lz_tx, oz_rx, lz_rx, att, hk, hy_tx, hy_rx, hz_tx, hz_rx,
-    load_sem, q_up, q_down, q_side, q_in, oy_out, oy_in, ly_out, ly_in,
+    load_sem, x_out, x_side, x_in, q_up, q_down, q_side, q_in, oy_out, oy_in, ly_out, ly_in,
     oz_out, oz_in, lz_out, lz_in, hy_out, hy_in, hz_out, hz_in,
     r_up, r_down, r_side, r_in,
 ):
     me = lax.axis_index("blk")
+    layer = lax.axis_index("segment")
+    layers = lax.axis_size("segment")
     z, y = me // 2, me % 2
     other = z * 2 + 1 - y
-    width = q_ref.shape[1]
+    tokens, width = qall.shape[1:]
     heads = width // HD
-    tokens = q_ref.shape[0]
-    scale = HD ** (-0.5)
-    to_exp2 = scale * math.log2(math.e)
+    to_log2 = HD ** (-0.5) * math.log2(math.e)
+    piece = tokens // PIECES
 
     def own_cols(c):
         return pl.ds(pl.multiple_of(c * width, width), width)
 
     loads = [
-        pltpu.make_async_copy(kc_hbm, kbuf, load_sem.at[0]),
-        pltpu.make_async_copy(vc_hbm, vbuf, load_sem.at[1]),
-        pltpu.make_async_copy(wo_hbm, wo, load_sem.at[2]),
-        pltpu.make_async_copy(cur_hbm.at[:, own_cols(me)], cur, load_sem.at[3]),
+        pltpu.make_async_copy(wq_hbm, wq, load_sem.at[0]),
+        pltpu.make_async_copy(wkv_hbm, wkv, load_sem.at[1]),
+        pltpu.make_async_copy(kc_hbm, kbuf, load_sem.at[2]),
+        pltpu.make_async_copy(vc_hbm, vbuf, load_sem.at[3]),
+        pltpu.make_async_copy(wo_hbm, wo, load_sem.at[4]),
     ]
+    fresh_load = pltpu.make_async_copy(fresh_hbm, cur, load_sem.at[5])
+
+    @pl.when(layer == 0)
+    def _():
+        fresh_load.start()
+
     for load in loads:
         load.start()
 
+    has_source, has_next = layer > 0, layer < layers - 1
     barrier = pltpu.get_barrier_semaphore()
     pl.semaphore_signal(barrier, inc=1, device_id={"blk": other}, device_id_type=MESH)
     for step in range(1, ROWS):
         pl.semaphore_signal(
             barrier, inc=1, device_id={"blk": near_first(z, step) * 2 + y}, device_id_type=MESH
         )
-    pl.semaphore_wait(barrier, ROWS)
+
+    @pl.when(has_source)
+    def _():
+        pl.semaphore_signal(
+            barrier, inc=1, device_id={"segment": layer - 1}, device_id_type=MESH
+        )
+
+    @pl.when(has_next)
+    def _():
+        pl.semaphore_signal(
+            barrier, inc=1, device_id={"segment": layer + 1}, device_id_type=MESH
+        )
+
+    pl.semaphore_wait(
+        barrier, ROWS + has_source.astype(jnp.int32) + has_next.astype(jnp.int32)
+    )
 
     def remote(src, dst, out_sem, in_sem, device):
         return pltpu.make_async_remote_copy(
@@ -221,6 +240,37 @@
             device_id={"blk": device}, device_id_type=MESH,
         )
 
+    def rows_of_piece(p):
+        return pl.ds(pl.multiple_of(p * piece, piece), piece)
+
+    def shift_copy(p):
+        rows = rows_of_piece(p)
+        return pltpu.make_async_remote_copy(
+            src_ref=prev_hbm.at[rows], dst_ref=cur.at[rows],
+            send_sem=x_out.at[p], recv_sem=x_in.at[p],
+            device_id={"segment": layer + 1}, device_id_type=MESH,
+        )
+
+    def shift_side(p):
+        rows = rows_of_piece(p)
+        return remote(cur.at[rows], cur.at[rows], x_side.at[p], x_in.at[p], other)
+
+    def piece_at(i):
+        return (y * (PIECES // 2) + i) % PIECES
+
+    to_core = layer % 2 == 0
+    takes_half = jnp.logical_and(has_source, to_core)
+
+    def each_shift(act):
+        def step(i, carry):
+            @pl.when(jnp.logical_and(has_next, jnp.logical_or(to_core, i < PIECES // 2)))
+            def _():
+                act(shift_copy(piece_at(i)))
+
+            return carry
+
+        lax.fori_loop(0, PIECES, step, 0)
+
     def spread(view, up, down, side, arrived, row, act):
         part = view(row * 2 + y)
         in_sem = arrived.at[row * 2 + y]
@@ -241,6 +291,8 @@
     def finish(copy):
         copy.wait_send()
 
+    each_shift(start)
+
     def q_view(c):
         return qall.at[c]
 
@@ -253,24 +305,69 @@
     def out_spread(row, act):
         spread(out_view, r_up, r_down, r_side, r_in, row, act)
 
-    lanes = lax.broadcasted_iota(jnp.int32, (tokens, HD), 1)
-
-    def one_head(q_part, k_part, v_part, bias):
+    slot_no = lax.broadcasted_iota(jnp.int32, bias.shape, 0)
+    bias[...] = jnp.where(slot_no < counts_ref[0, me], 0.0, -jnp.inf)
+
+    def normalize(i, carry):
+        p = piece_at(i)
+
+        @pl.when(has_source)
+        def _():
+            shift_side(p).wait_recv()
+
+        @pl.when(jnp.logical_and(takes_half, i < PIECES // 2))
+        def _():
+            shift_side(p).start()
+
+        @pl.when(jnp.logical_and(layer == 0, i == 0))
+        def _():
+            fresh_load.wait()
+
+        rows = rows_of_piece(p)
+        widened = cur[rows, :].astype(jnp.float32)
+        normed[rows, :] = (
+            widened
+            * lax.rsqrt(jnp.mean(widened * widened, axis=-1, keepdims=True) + EPSILON)
+            * gain_ref[...]
+        ).astype(jnp.bfloat16)
+        return carry
+
+    lax.fori_loop(0, PIECES, normalize, 0)
+
+    def rotated(part):
+        half = HD // 2
+        turned = jnp.concatenate([part[:, half:], part[:, :half]], axis=1)
+        return part * cos_ref[...] + turned * sin_ref[...]
+
+    loads[0].wait()
+    projected = jnp.dot(normed[...], wq[...], preferred_element_type=jnp.float32)
+    for h in range(heads):
+        cols = slice(h * HD, (h + 1) * HD)
+        qall[me, :, cols] = (rotated(projected[:, cols]) * to_log2).astype(jnp.bfloat16)
+
+    def one_head(k_part, q_part, v_turned, masked):
         scores = lax.dot_general(
-            q_part, k_part, (((1,), (1,)), ((), ())), preferred_element_type=jnp.float32
-        ) + bias
-        highest = jnp.max(scores, axis=-1, keepdims=True)
-        weights = jnp.exp2((scores - highest) * to_exp2)
-        totals = jnp.sum(weights, axis=-1, keepdims=True)
-        partial = jnp.dot(
-            weights.astype(jnp.bfloat16), v_part, preferred_element_type=jnp.float32
-        ) / totals
-        return partial.astype(jnp.bfloat16), highest * scale + jnp.log(totals)
+            k_part, q_part, (((1,), (1,)), ((), ())), preferred_element_type=jnp.float32
+        ) + masked
+        highest = jnp.max(scores, axis=0, keepdims=True)
+        weights = jnp.exp2(scores - highest).astype(jnp.bfloat16)
+        mixed = jnp.dot(v_turned, weights, preferred_element_type=jnp.float32)
+        totals = mixed[HD : HD + 1]
+        partial = (mixed[:HD] / totals).astype(jnp.bfloat16)
+        return partial, highest + jnp.log2(totals)
+
+    def with_ones(v_part):
+        return jnp.concatenate(
+            [v_part.T, jnp.ones((16, v_part.shape[0]), jnp.bfloat16)], axis=0
+        )
+
+    def log_rows(rows):
+        return jnp.concatenate(rows + [jnp.zeros((8 - heads, tokens), jnp.float32)], axis=0)
 
     def y_copies(row):
         return (
-            remote(oy_tx.at[row], oy_rx.at[row], oy_out.at[row], oy_in.at[row], other),
-            remote(ly_tx.at[row], ly_rx.at[row], ly_out.at[row], ly_in.at[row], other),
+            remote(parts.at[ROWS + row], oy_rx.at[row], oy_out.at[row], oy_in.at[row], other),
+            remote(logs.at[ROWS + row], ly_rx.at[row], ly_out.at[row], ly_in.at[row], other),
         )
 
     def z_copies(row):
@@ -283,25 +380,23 @@
     def merge(row, away):
         for copy in y_copies(row):
             copy.wait_recv()
-        l_a, l_b = l_keep[row], head_columns(ly_rx[row])
+        l_a, l_b = logs[row], ly_rx[row]
         top = jnp.maximum(l_a, l_b)
-        f_a, f_b = jnp.exp(l_a - top), jnp.exp(l_b - top)
+        f_a, f_b = jnp.exp2(l_a - top), jnp.exp2(l_b - top)
         total = f_a + f_b
         f_a, f_b = f_a / total, f_b / total
         o_dst, l_dst, at = (oz_tx, lz_tx, row) if away else (oz_rx, lz_rx, z)
-        l_dst[at] = head_rows(top + jnp.log(total))
+        l_dst[at] = top + jnp.log2(total)
         for h in range(heads):
-            cols = slice(h * HD, (h + 1) * HD)
-            o_dst[at, :, cols] = (
-                f_a[:, h : h + 1] * o_keep[row, :, cols].astype(jnp.float32)
-                + f_b[:, h : h + 1] * oy_rx[row, :, cols].astype(jnp.float32)
+            part = slice(h * HD, (h + 1) * HD)
+            o_dst[at, part, :] = (
+                f_a[h : h + 1] * parts[row, part, :].astype(jnp.float32)
+                + f_b[h : h + 1] * oy_rx[row, part, :].astype(jnp.float32)
             ).astype(jnp.bfloat16)
         if away:
             for copy in z_copies(row):
                 copy.start()
 
-    qall[me] = q_ref[...]
-
     def visit(t, carry):
         j, second = t // 2, t % 2
         row = near_first(z, j)
@@ -317,33 +412,28 @@
 
         @pl.when(t == 0)
         def _():
-            loads[0].wait()
             loads[1].wait()
+            both = jnp.dot(normed[...], wkv[...], preferred_element_type=jnp.float32)
+            own_k[...] = rotated(both[:, :HD]).astype(jnp.bfloat16)
+            own_v[...] = both[:, HD:].astype(jnp.bfloat16)
+            loads[2].wait()
+            loads[3].wait()
 
         group = pl.ds(pl.multiple_of(c * HD, HD), HD)
-        logs = jnp.zeros((tokens, HD), jnp.float32)
+        k_part, v_turned = kbuf[:, group], with_ones(vbuf[:, group])
+        masked = jnp.concatenate([bias[...]] * (tokens // HD), axis=1)
+        to = second * ROWS + row
+        totals = []
         for h in range(heads):
-            cols = slice(h * HD, (h + 1) * HD)
             partial, log_total = one_head(
-                qall[c, :, cols], kbuf[:, group], vbuf[:, group], bias_ref[...]
+                k_part, qall[c, :, h * HD : (h + 1) * HD], v_turned, masked
             )
-            logs = jnp.where(lanes == h, log_total, logs)
-
-            @pl.when(second == 0)
-            def _():
-                o_keep[row, :, cols] = partial
-
-            @pl.when(second == 1)
-            def _():
-                oy_tx[row, :, cols] = partial
-
-        @pl.when(second == 0)
-        def _():
-            l_keep[row] = logs
+            parts[to, h * HD : (h + 1) * HD, :] = partial
+            totals.append(log_total)
+        logs[to] = log_rows(totals)
 
         @pl.when(second == 1)
         def _():
-            ly_tx[row] = head_rows(logs)
             for copy in y_copies(row):
                 copy.start()
 
@@ -363,16 +453,16 @@
 
     lax.fori_loop(0, 2 * ROWS, visit, 0)
 
-    row_no = lax.broadcasted_iota(jnp.int32, (tokens, tokens), 0)
-    col_no = lax.broadcasted_iota(jnp.int32, (tokens, tokens), 1)
-    causal = jnp.where(row_no >= col_no, 0.0, -jnp.inf)
-    own = []
-    own_logs = jnp.zeros((tokens, HD), jnp.float32)
+    key_no = lax.broadcasted_iota(jnp.int32, (tokens, tokens), 0)
+    token_no = lax.broadcasted_iota(jnp.int32, (tokens, tokens), 1)
+    causal = jnp.where(token_no >= key_no, 0.0, -jnp.inf)
+    own, own_logs = [], []
+    own_turned = with_ones(own_v[...])
     for h in range(heads):
         partial, log_total = one_head(
-            q_ref[:, h * HD : (h + 1) * HD], ok_ref[...], ov_ref[...], causal
-        )
-        own_logs = jnp.where(lanes == h, log_total, own_logs)
+            own_k[...], qall[me, :, h * HD : (h + 1) * HD], own_turned, causal
+        )
+        own_logs.append(log_total)
         own.append(partial)
 
     merge(near_first(z, 3), True)
@@ -386,23 +476,23 @@
     for step in range(1, ROWS):
         for copy in from_row(near_first(z, step)):
             copy.wait_recv()
-    all_logs = [own_logs] + [head_columns(lz_rx[row]) for row in range(ROWS)]
+    all_logs = [log_rows(own_logs)] + [lz_rx[row] for row in range(ROWS)]
     top = all_logs[0]
-    for logs in all_logs[1:]:
-        top = jnp.maximum(top, logs)
-    factors = [jnp.exp(logs - top) for logs in all_logs]
+    for log_total in all_logs[1:]:
+        top = jnp.maximum(top, log_total)
+    factors = [jnp.exp2(log_total - top) for log_total in all_logs]
     total = factors[0]
     for factor in factors[1:]:
         total = total + factor
     factors = [factor / total for factor in factors]
     for h in range(heads):
-        cols = slice(h * HD, (h + 1) * HD)
-        summed = factors[0][:, h : h + 1] * own[h].astype(jnp.float32)
+        part = slice(h * HD, (h + 1) * HD)
+        summed = factors[0][h : h + 1] * own[h].astype(jnp.float32)
         for row in range(ROWS):
-            summed = summed + factors[row + 1][:, h : h + 1] * oz_rx[row, :, cols].astype(
+            summed = summed + factors[row + 1][h : h + 1] * oz_rx[row, part, :].astype(
                 jnp.float32
             )
-        att[:, cols] = summed.astype(jnp.bfloat16)
+        att[:, part] = summed.T.astype(jnp.bfloat16)
 
     def term(c):
         return jnp.dot(att[...], wo[:, own_cols(c)], preferred_element_type=jnp.float32)
@@ -413,8 +503,7 @@
     def row_terms(row, slot):
         return remote(hz_tx.at[row], hz_rx.at[slot], hz_out.at[row], hz_in.at[slot], row * 2 + y)
 
-    loads[2].wait()
-    loads[3].wait()
+    loads[4].wait()
 
     def send_side(i, carry):
         row = near_first(z, ROWS - 1 - i)
@@ -435,7 +524,7 @@
         hz_tx[row] = (hk[row] + hy_rx[row].astype(jnp.float32)).astype(jnp.bfloat16)
         row_terms(row, z).start()
     side_terms(z).wait_recv()
-    summed = cur[...].astype(jnp.float32) + hk[z] + hy_rx[z].astype(jnp.float32)
+    summed = cur[:, own_cols(me)].astype(jnp.float32) + hk[z] + hy_rx[z].astype(jnp.float32)
     for step in range(1, ROWS):
         row = near_first(z, step)
         row_terms(row, row).wait_recv()
@@ -452,6 +541,16 @@
         c = row * 2 + 1 - y
         remote(out_view(c), out_view(c), r_side.at[row], r_in.at[c], other).wait_recv()
 
+    each_shift(finish)
+
+    def side_done(i, carry):
+        @pl.when(takes_half)
+        def _():
+            shift_side(piece_at(i)).wait_send()
+
+        return carry
+
+    lax.fori_loop(0, PIECES // 2, side_done, 0)
     for row in range(ROWS):
         q_spread(row, finish)
         out_spread(row, finish)
@@ -465,75 +564,62 @@
         row_terms(row, z).wait_send()
 
 
-def plane_call(queries, own_keys, own_values, bias, current, keys, values, w_out):
-    tokens, width = queries.shape
+def plane_call(counts, gain, cosine, sine, fresh, previous, w_query, w_keyval, keys, values, w_out):
+    tokens, features = fresh.shape
+    width = w_query.shape[1]
     slots = keys.shape[0]
-    chunk = (tokens, width)
-    few = (ROWS, 8, tokens)
     bf16, f32 = jnp.bfloat16, jnp.float32
     vmem = pl.BlockSpec(memory_space=pltpu.VMEM)
     anywhere = pl.BlockSpec(memory_space=pl.ANY)
-    rows_of = lambda kind: pltpu.VMEM((ROWS,) + chunk, kind)
+    turned = lambda count: pltpu.VMEM((count, width, tokens), bf16)
+    chunks = lambda count, kind: pltpu.VMEM((count, tokens, width), kind)
+    logs = lambda count: pltpu.VMEM((count, 8, tokens), f32)
     sems = lambda count: pltpu.SemaphoreType.DMA((count,))
-    logs = pltpu.VMEM(few, f32)
+    like = lambda array: pltpu.VMEM(array.shape, array.dtype)
     return pl.pallas_call(
         plane_kernel,
-        out_shape=jax.ShapeDtypeStruct(current.shape, bf16),
-        in_specs=[vmem] * 4 + [anywhere] * 4,
+        out_shape=jax.ShapeDtypeStruct(fresh.shape, bf16),
+        in_specs=[pl.BlockSpec(memory_space=pltpu.SMEM)] + [vmem] * 3 + [anywhere] * 7,
         out_specs=vmem,
         scratch_shapes=[
-            pltpu.VMEM((2 * ROWS,) + chunk, bf16),
-            pltpu.VMEM(keys.shape, bf16),
-            pltpu.VMEM(values.shape, bf16),
-            pltpu.VMEM(w_out.shape, bf16),
-            pltpu.VMEM(chunk, bf16),
-            rows_of(bf16), pltpu.VMEM((ROWS, tokens, HD), f32),
-            rows_of(bf16), logs, rows_of(bf16), logs,
-            rows_of(bf16), logs, rows_of(bf16), logs,
-            pltpu.VMEM(chunk, bf16),
-            rows_of(f32), rows_of(bf16), rows_of(bf16), rows_of(bf16), rows_of(bf16),
-            sems(4),
+            like(fresh), like(fresh), like(w_query), like(w_keyval),
+            pltpu.VMEM((tokens, HD), bf16), pltpu.VMEM((tokens, HD), bf16),
+            pltpu.VMEM((slots, HD), f32),
+            chunks(2 * ROWS, bf16), like(keys), like(values), like(w_out),
+            turned(2 * ROWS), logs(2 * ROWS), turned(ROWS), logs(ROWS),
+            turned(ROWS), logs(ROWS), turned(ROWS), logs(ROWS),
+            pltpu.VMEM((tokens, width), bf16),
+            chunks(ROWS, f32), chunks(ROWS, bf16), chunks(ROWS, bf16),
+            chunks(ROWS, bf16), chunks(ROWS, bf16),
+            sems(6), sems(PIECES), sems(PIECES), sems(PIECES),
             sems(ROWS), sems(ROWS), sems(ROWS), sems(2 * ROWS),
         ] + [sems(ROWS)] * 12 + [
             sems(ROWS), sems(ROWS), sems(ROWS), sems(2 * ROWS),
         ],
         compiler_params=pltpu.CompilerParams(
-            collective_id=0, has_side_effects=True, vmem_limit_bytes=56 * 1024 * 1024
+            collective_id=0, has_side_effects=True, vmem_limit_bytes=60 * 1024 * 1024
         ),
         cost_estimate=pl.CostEstimate(
-            flops=4 * tokens * width * slots * 8, bytes_accessed=16 << 20,
+            flops=4 * tokens * width * slots * 8, bytes_accessed=20 << 20,
             transcendentals=tokens * slots * 32,
         ),
-    )(queries, own_keys, own_values, bias, current, keys, values, w_out)
+    )(counts, gain, cosine, sine, fresh, previous, w_query, w_keyval, keys, values, w_out)
 
 
 def plane_shards(
     fresh, previous, span_index, cache_counts, norm_gain,
     w_query, w_keyval, w_out, cache_keys, cache_values,
 ):
-    position = lax.axis_index("blk")
-    span_rows = fresh.shape[0]
-    arrived = passed_along(previous[0], "segment", 1)
-    current = jnp.where(lax.axis_index("segment") == 0, fresh, arrived)
-    widened = current.astype(jnp.float32)
-    normed = (
-        widened
-        * lax.rsqrt(jnp.mean(widened * widened, axis=-1, keepdims=True) + EPSILON)
-        * norm_gain[0]
-    ).astype(jnp.bfloat16)
-    first_span = span_index[0]
-    width = w_query.shape[2]
-    queries = jnp.dot(normed, w_query[0], preferred_element_type=jnp.float32)
-    queries = rotate(queries.reshape(span_rows, width // HD, HD), first_span)
-    queries = queries.astype(jnp.bfloat16).reshape(span_rows, width)
-    projected = jnp.dot(normed, w_keyval[0], preferred_element_type=jnp.float32)
-    own_keys = rotate(projected[:, None, :HD], first_span)[:, 0, :].astype(jnp.bfloat16)
-    own_values = projected[:, HD:].astype(jnp.bfloat16)
-    offsets = jnp.arange(cache_keys.shape[1], dtype=jnp.int32)
-    bias = jnp.where(offsets < cache_counts[0, position], 0.0, -jnp.inf)[None, :]
+    length = fresh.shape[0]
+    half_width = HD // 2
+    positions = (span_index[0] * length + jnp.arange(length, dtype=jnp.int32)).astype(jnp.float32)
+    inverse = ROPE_BASE ** (-(jnp.arange(half_width, dtype=jnp.float32) * 2.0) / HD)
+    angles = positions[:, None] * inverse[None, :]
+    cosine, sine = jnp.cos(angles), jnp.sin(angles)
     mixed = plane_call(
-        queries, own_keys, own_values, bias, current,
-        cache_keys[0], cache_values[0], w_out[0],
+        cache_counts, norm_gain,
+        jnp.concatenate([cosine, cosine], axis=1), jnp.concatenate([-sine, sine], axis=1),
+        fresh, previous[0], w_query[0], w_keyval[0], cache_keys[0], cache_values[0], w_out[0],
     )
     return mixed[None]
 

time: 172 us -> 162 us (0.942)
  the two profiles are of different devices: /device:TPU:1 before, /device:TPU:2 now
where the time goes in v2:
time: 162 us
  Pallas kernels  157 us (97%)
  local copies, waits for them, and re-layouts  3.13 us (2%)
    pallas_call x1, Pallas kernels, plane_call(): pl.pallas_call(plane_kernel, out_shape=jax.ShapeDtypeStruct(fresh.shape,...  157 us

profile of v2, /device:TPU:2, one launch (start us, length us, event | category | flops | bytes accessed | tf_op | source)
XLA Modules:
  0.0 161.7 jit_solution(13085826962128203010)
XLA Ops:
  0.7 0.5 fusion
  1.2 0.8 pad_maximum_fusion
  2.1 156.5 %shard_map.100 = bf16[256,4096]{1,0:T(8,128)(2,1)} custom-call(s32[1,8]{1,0:T(1,128)} %counts_ref.1, f32[1,4096]{1,0:T(1,128)} %gain_ref.1, f32[256,128]{1,0:T(8,128)} %get-tuple-element.8.cos_ref, f32[256,128]{1,0:T(8,128)} %get-tuple-element.9.sin_ref, bf16[256,4096]{1,0:T(8,128)(2,1)} %fresh_hbm.1, bf16[256,4096]{1,0:T(8,128)(2,1)} %bitcast.13, ...), custom_call_target="tpu_custom_call" | custom-call | flops 8589934592 | bytes 20971520 | tf_op jit(solution)/shard_map/pallas_call | solution.py:579
  158.6 3.1 %copy.13 = bf16[1,256,4096]{2,1,0:T(8,128)(2,1)} copy(bf16[1,256,4096]{2,1,0:T(8,128)(2,1)} %bitcast.8) | data formatting | bytes 4194304
  (2 shorter events, 0.0 us)

commit v3 on v2

--- a/solution.py
+++ b/solution.py
@@ -159,6 +159,9 @@
 
 ROWS = 4
 PIECES = 8
+BLOCKS = 4
+FINE = 4
+DEAD = -1e30
 MESH = pl.DeviceIdType.MESH
 
 
@@ -174,7 +177,7 @@
 def plane_kernel(
     counts_ref, gain_ref, cos_ref, sin_ref, fresh_hbm, prev_hbm, wq_hbm, wkv_hbm,
     kc_hbm, vc_hbm, wo_hbm, out_ref,
-    cur, normed, wq, wkv, own_k, own_v, bias,
+    cur, normed, wq, wkv, own_k, own_v, hidden, s_buf, p_buf, v_turn,
     qall, kbuf, vbuf, wo, parts, logs, oy_rx, ly_rx,
     oz_tx, lz_tx, oz_rx, lz_rx, att, hk, hy_tx, hy_rx, hz_tx, hz_rx,
     load_sem, x_out, x_side, x_in, q_up, q_down, q_side, q_in, oy_out, oy_in, ly_out, ly_in,
@@ -305,8 +308,16 @@
     def out_spread(row, act):
         spread(out_view, r_up, r_down, r_side, r_in, row, act)
 
-    slot_no = lax.broadcasted_iota(jnp.int32, bias.shape, 0)
-    bias[...] = jnp.where(slot_no < counts_ref[0, me], 0.0, -jnp.inf)
+    slot_no = lax.broadcasted_iota(jnp.int32, hidden.shape, 0)
+    lane_no = lax.broadcasted_iota(jnp.int32, hidden.shape, 1)
+    dead = jnp.logical_and(slot_no >= counts_ref[0, me], lane_no == 0)
+    hidden[...] = jnp.where(dead, DEAD, 0.0).astype(jnp.bfloat16)
+    v_turn[HD:, :] = jnp.ones((16, v_turn.shape[1]), jnp.bfloat16)
+    first_lane = jnp.where(
+        lax.broadcasted_iota(jnp.int32, (tokens, HD), 1) == 0, 1.0, 0.0
+    ).astype(jnp.bfloat16)
+    slots = hidden.shape[0]
+    block = slots // BLOCKS
 
     def normalize(i, carry):
         p = piece_at(i)
@@ -420,16 +431,54 @@
             loads[3].wait()
 
         group = pl.ds(pl.multiple_of(c * HD, HD), HD)
-        k_part, v_turned = kbuf[:, group], with_ones(vbuf[:, group])
-        masked = jnp.concatenate([bias[...]] * (tokens // HD), axis=1)
         to = second * ROWS + row
+        v_turn[:HD, :] = vbuf[:, group].T
+
+        def score_block(h, b, highest):
+            rows = slice(b * block, (b + 1) * block)
+            keys = jnp.concatenate([kbuf[rows, group], hidden[rows, :]], axis=1)
+            asked = jnp.concatenate(
+                [qall[c, :, h * HD : (h + 1) * HD], first_lane], axis=1
+            )
+            scores = lax.dot_general(
+                keys, asked, (((1,), (1,)), ((), ())), preferred_element_type=jnp.float32
+            )
+            s_buf[h % 2, rows, :] = scores
+            here = jnp.max(scores, axis=0, keepdims=True)
+            return here if highest is None else jnp.maximum(highest, here)
+
+        def weigh_block(h, b, highest):
+            fine = block // FINE
+            for i in range(FINE):
+                rows = slice(b * block + i * fine, b * block + (i + 1) * fine)
+                p_buf[h % 2, rows, :] = jnp.exp2(s_buf[h % 2, rows, :] - highest).astype(
+                    jnp.bfloat16
+                )
+
+        def value_block(h, b, total):
+            rows = slice(b * block, (b + 1) * block)
+            here = jnp.dot(
+                v_turn[:, rows], p_buf[h % 2, rows, :], preferred_element_type=jnp.float32
+            )
+            return here if total is None else total + here
+
         totals = []
+        highest = None
+        for b in range(BLOCKS):
+            highest = score_block(0, b, highest)
         for h in range(heads):
-            partial, log_total = one_head(
-                k_part, qall[c, :, h * HD : (h + 1) * HD], v_turned, masked
-            )
-            parts[to, h * HD : (h + 1) * HD, :] = partial
-            totals.append(log_total)
+            following, mixed = None, None
+            for b in range(BLOCKS):
+                if h + 1 < heads:
+                    following = score_block(h + 1, b, following)
+                weigh_block(h, b, highest)
+                if b > 0:
+                    mixed = value_block(h, b - 1, mixed)
+            mixed = value_block(h, BLOCKS - 1, mixed)
+            total = mixed[HD : HD + 1]
+            parts[to, h * HD : (h + 1) * HD, :] = (mixed[:HD] / total).astype(jnp.bfloat16)
+            totals.append(highest + jnp.log2(total))
+            highest = following
         logs[to] = log_rows(totals)
 
         @pl.when(second == 1)
@@ -584,7 +633,9 @@
         scratch_shapes=[
             like(fresh), like(fresh), like(w_query), like(w_keyval),
             pltpu.VMEM((tokens, HD), bf16), pltpu.VMEM((tokens, HD), bf16),
-            pltpu.VMEM((slots, HD), f32),
+            pltpu.VMEM((slots, HD), bf16),
+            pltpu.VMEM((2, slots, tokens), f32), pltpu.VMEM((2, slots, tokens), bf16),
+            pltpu.VMEM((HD + 16, slots), bf16),
             chunks(2 * ROWS, bf16), like(keys), like(values), like(w_out),
             turned(2 * ROWS), logs(2 * ROWS), turned(ROWS), logs(ROWS),
             turned(ROWS), logs(ROWS), turned(ROWS), logs(ROWS),

time: 162 us -> 155 us (0.957)
  Pallas kernels: 157 us -> 148 us
    pallas_call x1, Pallas kernels: 157 us -> 148 us  [plane_call(): pl.pallas_call(plane_kernel, out_shape=jax.ShapeDtypeStruct(fresh.shape,...]
where the time goes in v3:
time: 155 us; the launch traced here: 154 us
  Pallas kernels  148 us (95%)
  local copies, waits for them, and re-layouts  3.13 us (2%)
    pallas_call x1, Pallas kernels, plane_call(): pl.pallas_call(plane_kernel, out_shape=jax.ShapeDtypeStruct(fresh.shape,...  148 us
    unnamed x1, local copies, waits for them, and re-layouts  3.13 us

profile of v3, /device:TPU:2, one launch (start us, length us, event | category | flops | bytes accessed | tf_op | source)
XLA Modules:
  0.0 153.6 jit_solution(15998722697873856363)
XLA Ops:
  0.7 0.5 fusion
  1.2 0.8 pad_maximum_fusion
  2.1 148.4 %shard_map.100 = bf16[256,4096]{1,0:T(8,128)(2,1)} custom-call(s32[1,8]{1,0:T(1,128)} %counts_ref.1, f32[1,4096]{1,0:T(1,128)} %gain_ref.1, f32[256,128]{1,0:T(8,128)} %get-tuple-element.8.cos_ref, f32[256,128]{1,0:T(8,128)} %get-tuple-element.9.sin_ref, bf16[256,4096]{1,0:T(8,128)(2,1)} %fresh_hbm.1, bf16[256,4096]{1,0:T(8,128)(2,1)} %bitcast.13, ...), custom_call_target="tpu_custom_call" | custom-call | flops 8589934592 | bytes 20971520 | tf_op jit(solution)/shard_map/pallas_call | solution.py:628
  150.5 3.1 %copy.13 = bf16[1,256,4096]{2,1,0:T(8,128)(2,1)} copy(bf16[1,256,4096]{2,1,0:T(8,128)(2,1)} %bitcast.8) | data formatting | bytes 4194304
  (2 shorter events, 0.0 us)

commit v4 on v3

--- a/solution.py
+++ b/solution.py
@@ -189,7 +189,7 @@
     layers = lax.axis_size("segment")
     z, y = me // 2, me % 2
     other = z * 2 + 1 - y
-    tokens, width = qall.shape[1:]
+    width, tokens = qall.shape[1:]
     heads = width // HD
     to_log2 = HD ** (-0.5) * math.log2(math.e)
     piece = tokens // PIECES
@@ -312,9 +312,10 @@
     lane_no = lax.broadcasted_iota(jnp.int32, hidden.shape, 1)
     dead = jnp.logical_and(slot_no >= counts_ref[0, me], lane_no == 0)
     hidden[...] = jnp.where(dead, DEAD, 0.0).astype(jnp.bfloat16)
-    v_turn[HD:, :] = jnp.ones((16, v_turn.shape[1]), jnp.bfloat16)
-    first_lane = jnp.where(
-        lax.broadcasted_iota(jnp.int32, (tokens, HD), 1) == 0, 1.0, 0.0
+    for slot in range(2):
+        v_turn[slot, HD:, :] = jnp.ones((16, v_turn.shape[2]), jnp.bfloat16)
+    first_row = jnp.where(
+        lax.broadcasted_iota(jnp.int32, (HD, tokens), 0) == 0, 1.0, 0.0
     ).astype(jnp.bfloat16)
     slots = hidden.shape[0]
     block = slots // BLOCKS
@@ -354,12 +355,10 @@
     projected = jnp.dot(normed[...], wq[...], preferred_element_type=jnp.float32)
     for h in range(heads):
         cols = slice(h * HD, (h + 1) * HD)
-        qall[me, :, cols] = (rotated(projected[:, cols]) * to_log2).astype(jnp.bfloat16)
+        qall[me, cols, :] = (rotated(projected[:, cols]) * to_log2).T.astype(jnp.bfloat16)
 
     def one_head(k_part, q_part, v_turned, masked):
-        scores = lax.dot_general(
-            k_part, q_part, (((1,), (1,)), ((), ())), preferred_element_type=jnp.float32
-        ) + masked
+        scores = jnp.dot(k_part, q_part, preferred_element_type=jnp.float32) + masked
         highest = jnp.max(scores, axis=0, keepdims=True)
         weights = jnp.exp2(scores - highest).astype(jnp.bfloat16)
         mixed = jnp.dot(v_turned, weights, preferred_element_type=jnp.float32)
@@ -408,41 +407,50 @@
             for copy in z_copies(row):
                 copy.start()
 
+    def chunk_at(t):
+        row = near_first(z, t // 2)
+        return row, row * 2 + jnp.where(t % 2 == 0, y, 1 - y)
+
+    def group_of(c):
+        return pl.ds(pl.multiple_of(c * HD, HD), HD)
+
+    def turn_values(c, slot, b):
+        rows = slice(b * block, (b + 1) * block)
+        v_turn[slot, :HD, rows] = vbuf[rows, group_of(c)].T
+
+    q_spread(z, start)
+    loads[1].wait()
+    both = jnp.dot(normed[...], wkv[...], preferred_element_type=jnp.float32)
+    own_k[...] = rotated(both[:, :HD]).astype(jnp.bfloat16)
+    own_v[...] = both[:, HD:].astype(jnp.bfloat16)
+    loads[2].wait()
+    loads[3].wait()
+    for b in range(BLOCKS):
+        turn_values(me, 0, b)
+
     def visit(t, carry):
-        j, second = t // 2, t % 2
-        row = near_first(z, j)
-        c = row * 2 + jnp.where(second == 0, y, 1 - y)
+        second = t % 2
+        row, c = chunk_at(t)
+        following_c = chunk_at(t + 1)[1]
 
         @pl.when(t > 0)
         def _():
             remote(q_view(c), q_view(c), q_side.at[row], q_in.at[c], other).wait_recv()
 
-        @pl.when(second == 0)
+        @pl.when(jnp.logical_and(t > 0, second == 0))
         def _():
             q_spread(row, start)
 
-        @pl.when(t == 0)
-        def _():
-            loads[1].wait()
-            both = jnp.dot(normed[...], wkv[...], preferred_element_type=jnp.float32)
-            own_k[...] = rotated(both[:, :HD]).astype(jnp.bfloat16)
-            own_v[...] = both[:, HD:].astype(jnp.bfloat16)
-            loads[2].wait()
-            loads[3].wait()
-
-        group = pl.ds(pl.multiple_of(c * HD, HD), HD)
+        group = group_of(c)
         to = second * ROWS + row
-        v_turn[:HD, :] = vbuf[:, group].T
 
         def score_block(h, b, highest):
             rows = slice(b * block, (b + 1) * block)
             keys = jnp.concatenate([kbuf[rows, group], hidden[rows, :]], axis=1)
             asked = jnp.concatenate(
-                [qall[c, :, h * HD : (h + 1) * HD], first_lane], axis=1
+                [qall[c, h * HD : (h + 1) * HD, :], first_row], axis=0
             )
-            scores = lax.dot_general(
-                keys, asked, (((1,), (1,)), ((), ())), preferred_element_type=jnp.float32
-            )
+            scores = jnp.dot(keys, asked, preferred_element_type=jnp.float32)
             s_buf[h % 2, rows, :] = scores
             here = jnp.max(scores, axis=0, keepdims=True)
             return here if highest is None else jnp.maximum(highest, here)
@@ -458,7 +466,7 @@
         def value_block(h, b, total):
             rows = slice(b * block, (b + 1) * block)
             here = jnp.dot(
-                v_turn[:, rows], p_buf[h % 2, rows, :], preferred_element_type=jnp.float32
+                v_turn[second, :, rows], p_buf[h % 2, rows, :], preferred_element_type=jnp.float32
             )
             return here if total is None else total + here
 
@@ -472,6 +480,8 @@
                 if h + 1 < heads:
                     following = score_block(h + 1, b, following)
                 weigh_block(h, b, highest)
+                if b == heads - 1 - h:
+                    turn_values(following_c, 1 - second, h)
                 if b > 0:
                     mixed = value_block(h, b - 1, mixed)
             mixed = value_block(h, BLOCKS - 1, mixed)
@@ -509,7 +519,7 @@
     own_turned = with_ones(own_v[...])
     for h in range(heads):
         partial, log_total = one_head(
-            own_k[...], qall[me, :, h * HD : (h + 1) * HD], own_turned, causal
+            own_k[...], qall[me, h * HD : (h + 1) * HD, :], own_turned, causal
         )
         own_logs.append(log_total)
         own.append(partial)
@@ -635,8 +645,8 @@
             pltpu.VMEM((tokens, HD), bf16), pltpu.VMEM((tokens, HD), bf16),
             pltpu.VMEM((slots, HD), bf16),
             pltpu.VMEM((2, slots, tokens), f32), pltpu.VMEM((2, slots, tokens), bf16),
-            pltpu.VMEM((HD + 16, slots), bf16),
-            chunks(2 * ROWS, bf16), like(keys), like(values), like(w_out),
+            pltpu.VMEM((2, HD + 16, slots), bf16),
+            turned(2 * ROWS), like(keys), like(values), like(w_out),
             turned(2 * ROWS), logs(2 * ROWS), turned(ROWS), logs(ROWS),
             turned(ROWS), logs(ROWS), turned(ROWS), logs(ROWS),
             pltpu.VMEM((tokens, width), bf16),

time: 155 us -> 154 us (level); the launches traced: 154 us -> 154 us
  no operation moved by 1% of the time
where the time goes in v4:
time: 154 us
  Pallas kernels  149 us (97%)
  local copies, waits for them, and re-layouts  3.13 us (2%)
    pallas_call x1, Pallas kernels, plane_call(): pl.pallas_call(plane_kernel, out_shape=jax.ShapeDtypeStruct(fresh.shape,...  149 us
    unnamed x1, local copies, waits for them, and re-layouts  3.13 us

profile of v4, /device:TPU:2, one launch (start us, length us, event | category | flops | bytes accessed | tf_op | source)
XLA Modules:
  0.0 154.2 jit_solution(7689638513122321442)
XLA Ops:
  0.7 0.5 fusion
  1.2 0.8 pad_maximum_fusion
  2.1 149.0 %shard_map.100 = bf16[256,4096]{1,0:T(8,128)(2,1)} custom-call(s32[1,8]{1,0:T(1,128)} %counts_ref.1, f32[1,4096]{1,0:T(1,128)} %gain_ref.1, f32[256,128]{1,0:T(8,128)} %get-tuple-element.8.cos_ref, f32[256,128]{1,0:T(8,128)} %get-tuple-element.9.sin_ref, bf16[256,4096]{1,0:T(8,128)(2,1)} %fresh_hbm.1, bf16[256,4096]{1,0:T(8,128)(2,1)} %bitcast.13, ...), custom_call_target="tpu_custom_call" | custom-call | flops 8589934592 | bytes 20971520 | tf_op jit(solution)/shard_map/pallas_call | solution.py:638
  151.1 3.1 %copy.13 = bf16[1,256,4096]{2,1,0:T(8,128)(2,1)} copy(bf16[1,256,4096]{2,1,0:T(8,128)(2,1)} %bitcast.8) | data formatting | bytes 4194304
  (2 shorter events, 0.0 us)

commit v5 on v4

--- a/solution.py
+++ b/solution.py
@@ -159,6 +159,8 @@
 
 ROWS = 4
 PIECES = 8
+PAIR = 2
+HALVES = 2
 BLOCKS = 4
 FINE = 4
 DEAD = -1e30
@@ -189,7 +191,7 @@
     layers = lax.axis_size("segment")
     z, y = me // 2, me % 2
     other = z * 2 + 1 - y
-    width, tokens = qall.shape[1:]
+    tokens, width = cur.shape[0], wq.shape[1]
     heads = width // HD
     to_log2 = HD ** (-0.5) * math.log2(math.e)
     piece = tokens // PIECES
@@ -274,19 +276,20 @@
 
         lax.fori_loop(0, PIECES, step, 0)
 
-    def spread(view, up, down, side, arrived, row, act):
-        part = view(row * 2 + y)
-        in_sem = arrived.at[row * 2 + y]
+    def spread(view, up, down, side, arrived, row, act, half=0):
+        part = view(row * 2 + y, half)
+        in_sem = arrived.at[half * 2 * ROWS + row * 2 + y]
+        slot = half * ROWS + row
 
         @pl.when(jnp.logical_and(row <= z, z < ROWS - 1))
         def _():
-            act(remote(part, part, up.at[row], in_sem, me + 2))
+            act(remote(part, part, up.at[slot], in_sem, me + 2))
 
         @pl.when(jnp.logical_and(row >= z, z > 0))
         def _():
-            act(remote(part, part, down.at[row], in_sem, me - 2))
-
-        act(remote(part, part, side.at[row], in_sem, other))
+            act(remote(part, part, down.at[slot], in_sem, me - 2))
+
+        act(remote(part, part, side.at[slot], in_sem, other))
 
     def start(copy):
         copy.start()
@@ -296,17 +299,20 @@
 
     each_shift(start)
 
-    def q_view(c):
+    def q_view(c, half=0):
         return qall.at[c]
 
-    def out_view(c):
-        return out_ref.at[:, own_cols(c)]
+    def half_rows(half):
+        return pl.ds(half * (tokens // HALVES), tokens // HALVES)
+
+    def out_view(c, half):
+        return out_ref.at[half_rows(half), own_cols(c)]
 
     def q_spread(row, act):
         spread(q_view, q_up, q_down, q_side, q_in, row, act)
 
-    def out_spread(row, act):
-        spread(out_view, r_up, r_down, r_side, r_in, row, act)
+    def out_spread(row, act, half):
+        spread(out_view, r_up, r_down, r_side, r_in, row, act, half)
 
     slot_no = lax.broadcasted_iota(jnp.int32, hidden.shape, 0)
     lane_no = lax.broadcasted_iota(jnp.int32, hidden.shape, 1)
@@ -315,7 +321,7 @@
     for slot in range(2):
         v_turn[slot, HD:, :] = jnp.ones((16, v_turn.shape[2]), jnp.bfloat16)
     first_row = jnp.where(
-        lax.broadcasted_iota(jnp.int32, (HD, tokens), 0) == 0, 1.0, 0.0
+        lax.broadcasted_iota(jnp.int32, (HD, PAIR * tokens), 0) == 0, 1.0, 0.0
     ).astype(jnp.bfloat16)
     slots = hidden.shape[0]
     block = slots // BLOCKS
@@ -355,7 +361,7 @@
     projected = jnp.dot(normed[...], wq[...], preferred_element_type=jnp.float32)
     for h in range(heads):
         cols = slice(h * HD, (h + 1) * HD)
-        qall[me, cols, :] = (rotated(projected[:, cols]) * to_log2).T.astype(jnp.bfloat16)
+        qall[me, :, h * tokens : (h + 1) * tokens] = (rotated(projected[:, cols]) * to_log2).T.astype(jnp.bfloat16)
 
     def one_head(k_part, q_part, v_turned, masked):
         scores = jnp.dot(k_part, q_part, preferred_element_type=jnp.float32) + masked
@@ -398,10 +404,10 @@
         o_dst, l_dst, at = (oz_tx, lz_tx, row) if away else (oz_rx, lz_rx, z)
         l_dst[at] = top + jnp.log2(total)
         for h in range(heads):
-            part = slice(h * HD, (h + 1) * HD)
-            o_dst[at, part, :] = (
-                f_a[h : h + 1] * parts[row, part, :].astype(jnp.float32)
-                + f_b[h : h + 1] * oy_rx[row, part, :].astype(jnp.float32)
+            part = slice(h * tokens, (h + 1) * tokens)
+            o_dst[at, :, part] = (
+                f_a[h : h + 1] * parts[row, :, part].astype(jnp.float32)
+                + f_b[h : h + 1] * oy_rx[row, :, part].astype(jnp.float32)
             ).astype(jnp.bfloat16)
         if away:
             for copy in z_copies(row):
@@ -443,12 +449,13 @@
 
         group = group_of(c)
         to = second * ROWS + row
+        wide, pairs = PAIR * tokens, heads // PAIR
 
         def score_block(h, b, highest):
             rows = slice(b * block, (b + 1) * block)
             keys = jnp.concatenate([kbuf[rows, group], hidden[rows, :]], axis=1)
             asked = jnp.concatenate(
-                [qall[c, h * HD : (h + 1) * HD, :], first_row], axis=0
+                [qall[c, :, h * wide : (h + 1) * wide], first_row], axis=0
             )
             scores = jnp.dot(keys, asked, preferred_element_type=jnp.float32)
             s_buf[h % 2, rows, :] = scores
@@ -474,20 +481,21 @@
         highest = None
         for b in range(BLOCKS):
             highest = score_block(0, b, highest)
-        for h in range(heads):
+        for h in range(pairs):
             following, mixed = None, None
             for b in range(BLOCKS):
-                if h + 1 < heads:
+                if h + 1 < pairs:
                     following = score_block(h + 1, b, following)
                 weigh_block(h, b, highest)
-                if b == heads - 1 - h:
-                    turn_values(following_c, 1 - second, h)
+                if b % pairs == h:
+                    turn_values(following_c, 1 - second, b)
                 if b > 0:
                     mixed = value_block(h, b - 1, mixed)
             mixed = value_block(h, BLOCKS - 1, mixed)
             total = mixed[HD : HD + 1]
-            parts[to, h * HD : (h + 1) * HD, :] = (mixed[:HD] / total).astype(jnp.bfloat16)
-            totals.append(highest + jnp.log2(total))
+            parts[to, :, h * wide : (h + 1) * wide] = (mixed[:HD] / total).astype(jnp.bfloat16)
+            log_total = highest + jnp.log2(total)
+            totals += [log_total[:, i * tokens : (i + 1) * tokens] for i in range(PAIR)]
             highest = following
         logs[to] = log_rows(totals)
 
@@ -519,7 +527,7 @@
     own_turned = with_ones(own_v[...])
     for h in range(heads):
         partial, log_total = one_head(
-            own_k[...], qall[me, h * HD : (h + 1) * HD, :], own_turned, causal
+            own_k[...], qall[me, :, h * tokens : (h + 1) * tokens], own_turned, causal
         )
         own_logs.append(log_total)
         own.append(partial)
@@ -545,29 +553,36 @@
         total = total + factor
     factors = [factor / total for factor in factors]
     for h in range(heads):
-        part = slice(h * HD, (h + 1) * HD)
+        part = slice(h * tokens, (h + 1) * tokens)
         summed = factors[0][h : h + 1] * own[h].astype(jnp.float32)
         for row in range(ROWS):
-            summed = summed + factors[row + 1][h : h + 1] * oz_rx[row, part, :].astype(
+            summed = summed + factors[row + 1][h : h + 1] * oz_rx[row, :, part].astype(
                 jnp.float32
             )
-        att[:, part] = summed.T.astype(jnp.bfloat16)
+        att[:, h * HD : (h + 1) * HD] = summed.T.astype(jnp.bfloat16)
 
     def term(c):
         return jnp.dot(att[...], wo[:, own_cols(c)], preferred_element_type=jnp.float32)
 
-    def side_terms(row):
-        return remote(hy_tx.at[row], hy_rx.at[row], hy_out.at[row], hy_in.at[row], other)
-
-    def row_terms(row, slot):
-        return remote(hz_tx.at[row], hz_rx.at[slot], hz_out.at[row], hz_in.at[slot], row * 2 + y)
+    def side_terms(row, half):
+        rows, slot = half_rows(half), half * ROWS + row
+        return remote(
+            hy_tx.at[row, rows], hy_rx.at[row, rows], hy_out.at[slot], hy_in.at[slot], other
+        )
+
+    def row_terms(row, at, half):
+        rows = half_rows(half)
+        return remote(
+            hz_tx.at[row, rows], hz_rx.at[at, rows],
+            hz_out.at[half * ROWS + row], hz_in.at[half * ROWS + at], row * 2 + y,
+        )
 
     loads[4].wait()
 
     def send_side(i, carry):
         row = near_first(z, ROWS - 1 - i)
         hy_tx[row] = term(row * 2 + 1 - y).astype(jnp.bfloat16)
-        side_terms(row).start()
+        side_terms(row, 0).start()
         return carry
 
     def keep_own(i, carry):
@@ -576,29 +591,57 @@
         return carry
 
     lax.fori_loop(0, ROWS, send_side, 0)
+    for half in range(1, HALVES):
+        for step in range(ROWS - 1, -1, -1):
+            side_terms(near_first(z, step), half).start()
     lax.fori_loop(0, ROWS, keep_own, 0)
+
+    def reduce_row(step, half):
+        row, rows = near_first(z, step), half_rows(half)
+        side_terms(row, half).wait_recv()
+        hz_tx[row, rows, :] = (
+            hk[row, rows, :] + hy_rx[row, rows, :].astype(jnp.float32)
+        ).astype(jnp.bfloat16)
+        row_terms(row, z, half).start()
+
+    def settle(half):
+        rows = half_rows(half)
+        side_terms(z, half).wait_recv()
+        summed = (
+            cur[rows, own_cols(me)].astype(jnp.float32)
+            + hk[z, rows, :]
+            + hy_rx[z, rows, :].astype(jnp.float32)
+        )
+        for step in range(1, ROWS):
+            row = near_first(z, step)
+            row_terms(row, row, half).wait_recv()
+            summed = summed + hz_rx[row, rows, :].astype(jnp.float32)
+        out_ref[rows, own_cols(me)] = summed.astype(jnp.bfloat16)
+        out_spread(z, start, half)
+
+    def out_arrived(c, half):
+        view = out_view(c, half)
+        in_sem = r_in.at[half * 2 * ROWS + c]
+        remote(view, view, r_side.at[0], in_sem, other).wait_recv()
+
+    def pass_on(step, half):
+        row = near_first(z, step)
+        out_arrived(row * 2 + y, half)
+        out_spread(row, start, half)
+
     for step in range(ROWS - 1, 0, -1):
-        row = near_first(z, step)
-        side_terms(row).wait_recv()
-        hz_tx[row] = (hk[row] + hy_rx[row].astype(jnp.float32)).astype(jnp.bfloat16)
-        row_terms(row, z).start()
-    side_terms(z).wait_recv()
-    summed = cur[:, own_cols(me)].astype(jnp.float32) + hk[z] + hy_rx[z].astype(jnp.float32)
+        reduce_row(step, 0)
+    settle(0)
+    for half in range(1, HALVES):
+        for step in range(ROWS - 1, 0, -1):
+            reduce_row(step, half)
+            pass_on(ROWS - step, half - 1)
+        settle(half)
     for step in range(1, ROWS):
-        row = near_first(z, step)
-        row_terms(row, row).wait_recv()
-        summed = summed + hz_rx[row].astype(jnp.float32)
-    out_ref[:, own_cols(me)] = summed.astype(jnp.bfloat16)
-
-    out_spread(z, start)
-    for step in range(1, ROWS):
-        row = near_first(z, step)
-        c = row * 2 + y
-        remote(out_view(c), out_view(c), r_side.at[row], r_in.at[c], other).wait_recv()
-        out_spread(row, start)
-    for row in range(ROWS):
-        c = row * 2 + 1 - y
-        remote(out_view(c), out_view(c), r_side.at[row], r_in.at[c], other).wait_recv()
+        pass_on(step, HALVES - 1)
+    for half in range(HALVES):
+        for row in range(ROWS):
+            out_arrived(row * 2 + 1 - y, half)
 
     each_shift(finish)
 
@@ -612,15 +655,17 @@
     lax.fori_loop(0, PIECES // 2, side_done, 0)
     for row in range(ROWS):
         q_spread(row, finish)
-        out_spread(row, finish)
-        side_terms(row).wait_send()
+        for half in range(HALVES):
+            out_spread(row, finish, half)
+            side_terms(row, half).wait_send()
         for copy in y_copies(row):
             copy.wait_send()
     for step in range(1, ROWS):
         row = near_first(z, step)
         for copy in z_copies(row):
             copy.wait_send()
-        row_terms(row, z).wait_send()
+        for half in range(HALVES):
+            row_terms(row, z, half).wait_send()
 
 
 def plane_call(counts, gain, cosine, sine, fresh, previous, w_query, w_keyval, keys, values, w_out):
@@ -630,7 +675,7 @@
     bf16, f32 = jnp.bfloat16, jnp.float32
     vmem = pl.BlockSpec(memory_space=pltpu.VMEM)
     anywhere = pl.BlockSpec(memory_space=pl.ANY)
-    turned = lambda count: pltpu.VMEM((count, width, tokens), bf16)
+    turned = lambda count: pltpu.VMEM((count, HD, width // HD * tokens), bf16)
     chunks = lambda count, kind: pltpu.VMEM((count, tokens, width), kind)
     logs = lambda count: pltpu.VMEM((count, 8, tokens), f32)
     sems = lambda count: pltpu.SemaphoreType.DMA((count,))
@@ -644,7 +689,8 @@
             like(fresh), like(fresh), like(w_query), like(w_keyval),
             pltpu.VMEM((tokens, HD), bf16), pltpu.VMEM((tokens, HD), bf16),
             pltpu.VMEM((slots, HD), bf16),
-            pltpu.VMEM((2, slots, tokens), f32), pltpu.VMEM((2, slots, tokens), bf16),
+            pltpu.VMEM((2, slots, PAIR * tokens), f32),
+            pltpu.VMEM((2, slots, PAIR * tokens), bf16),
             pltpu.VMEM((2, HD + 16, slots), bf16),
             turned(2 * ROWS), like(keys), like(values), like(w_out),
             turned(2 * ROWS), logs(2 * ROWS), turned(ROWS), logs(ROWS),
@@ -654,9 +700,7 @@
             chunks(ROWS, bf16), chunks(ROWS, bf16),
             sems(6), sems(PIECES), sems(PIECES), sems(PIECES),
             sems(ROWS), sems(ROWS), sems(ROWS), sems(2 * ROWS),
-        ] + [sems(ROWS)] * 12 + [
-            sems(ROWS), sems(ROWS), sems(ROWS), sems(2 * ROWS),
-        ],
+        ] + [sems(ROWS)] * 8 + [sems(HALVES * ROWS)] * 7 + [sems(2 * HALVES * ROWS)],
         compiler_params=pltpu.CompilerParams(
             collective_id=0, has_side_effects=True, vmem_limit_bytes=60 * 1024 * 1024
         ),

time: 154 us -> 157 us (1.019)
  Pallas kernels: 149 us -> 152 us
    pallas_call x1, Pallas kernels: 149 us -> 152 us  [plane_call(): pl.pallas_call(plane_kernel, out_shape=jax.ShapeDtypeStruct(fresh.shape,...]
where the time goes in v5:
time: 157 us
  Pallas kernels  152 us (97%)
  local copies, waits for them, and re-layouts  3.13 us (2%)
    pallas_call x1, Pallas kernels, plane_call(): pl.pallas_call(plane_kernel, out_shape=jax.ShapeDtypeStruct(fresh.shape,...  152 us

profile of v5, /device:TPU:2, one launch (start us, length us, event | category | flops | bytes accessed | tf_op | source)
XLA Modules:
  0.0 157.2 jit_solution(348957316921479604)
XLA Ops:
  0.7 0.5 fusion
  1.2 0.8 pad_maximum_fusion
  2.1 152.0 %shard_map.100 = bf16[256,4096]{1,0:T(8,128)(2,1)} custom-call(s32[1,8]{1,0:T(1,128)} %counts_ref.1, f32[1,4096]{1,0:T(1,128)} %gain_ref.1, f32[256,128]{1,0:T(8,128)} %get-tuple-element.8.cos_ref, f32[256,128]{1,0:T(8,128)} %get-tuple-element.9.sin_ref, bf16[256,4096]{1,0:T(8,128)(2,1)} %fresh_hbm.1, bf16[256,4096]{1,0:T(8,128)(2,1)} %bitcast.13, ...), custom_call_target="tpu_custom_call" | custom-call | flops 8589934592 | bytes 20971520 | tf_op jit(solution)/shard_map/pallas_call | solution.py:683
  154.0 3.1 %copy.13 = bf16[1,256,4096]{2,1,0:T(8,128)(2,1)} copy(bf16[1,256,4096]{2,1,0:T(8,128)(2,1)} %bitcast.8) | data formatting | bytes 4194304
  (2 shorter events, 0.0 us)

commit v6 on v5

--- a/solution.py
+++ b/solution.py
@@ -160,7 +160,7 @@
 ROWS = 4
 PIECES = 8
 PAIR = 2
-HALVES = 2
+HALVES = 1
 BLOCKS = 4
 FINE = 4
 DEAD = -1e30
@@ -466,9 +466,8 @@
             fine = block // FINE
             for i in range(FINE):
                 rows = slice(b * block + i * fine, b * block + (i + 1) * fine)
-                p_buf[h % 2, rows, :] = jnp.exp2(s_buf[h % 2, rows, :] - highest).astype(
-                    jnp.bfloat16
-                )
+                lowered = (s_buf[h % 2, rows, :] - highest).astype(jnp.bfloat16)
+                p_buf[h % 2, rows, :] = jnp.exp2(lowered)
 
         def value_block(h, b, total):
             rows = slice(b * block, (b + 1) * block)

time: 157 us -> 157 us (level)
  no operation moved by 1% of the time
where the time goes in v6:
time: 157 us; the launch traced here: 156 us
  Pallas kernels  151 us (96%)
  local copies, waits for them, and re-layouts  3.13 us (2%)
    pallas_call x1, Pallas kernels, plane_call(): pl.pallas_call(plane_kernel, out_shape=jax.ShapeDtypeStruct(fresh.shape,...  151 us

profile of v6, /device:TPU:2, one launch (start us, length us, event | category | flops | bytes accessed | tf_op | source)
XLA Modules:
  0.0 156.2 jit_solution(17647283559834772144)
XLA Ops:
  0.7 0.5 fusion
  1.2 0.8 pad_maximum_fusion
  2.1 151.0 %shard_map.100 = bf16[256,4096]{1,0:T(8,128)(2,1)} custom-call(s32[1,8]{1,0:T(1,128)} %counts_ref.1, f32[1,4096]{1,0:T(1,128)} %gain_ref.1, f32[256,128]{1,0:T(8,128)} %get-tuple-element.8.cos_ref, f32[256,128]{1,0:T(8,128)} %get-tuple-element.9.sin_ref, bf16[256,4096]{1,0:T(8,128)(2,1)} %fresh_hbm.1, bf16[256,4096]{1,0:T(8,128)(2,1)} %bitcast.13, ...), custom_call_target="tpu_custom_call" | custom-call | flops 8589934592 | bytes 20971520 | tf_op jit(solution)/shard_map/pallas_call | solution.py:682
  153.1 3.1 %copy.13 = bf16[1,256,4096]{2,1,0:T(8,128)(2,1)} copy(bf16[1,256,4096]{2,1,0:T(8,128)(2,1)} %bitcast.8) | data formatting | bytes 4194304
  (2 shorter events, 0.0 us)

commit v7 on v5

--- a/solution.py
+++ b/solution.py
@@ -159,7 +159,7 @@
 
 ROWS = 4
 PIECES = 8
-PAIR = 2
+PAIR = 1
 HALVES = 2
 BLOCKS = 4
 FINE = 4
@@ -414,8 +414,9 @@
                 copy.start()
 
     def chunk_at(t):
-        row = near_first(z, t // 2)
-        return row, row * 2 + jnp.where(t % 2 == 0, y, 1 - y)
+        row = near_first(z, (t + 1) // 2 % ROWS)
+        second = jnp.where(t == 0, 0, jnp.where(t == 2 * ROWS - 1, 1, (t + 1) % 2))
+        return row, row * 2 + jnp.where(second == 0, y, 1 - y), second
 
     def group_of(c):
         return pl.ds(pl.multiple_of(c * HD, HD), HD)
@@ -435,8 +436,8 @@
         turn_values(me, 0, b)
 
     def visit(t, carry):
-        second = t % 2
-        row, c = chunk_at(t)
+        slot = t % 2
+        row, c, second = chunk_at(t)
         following_c = chunk_at(t + 1)[1]
 
         @pl.when(t > 0)
@@ -473,7 +474,7 @@
         def value_block(h, b, total):
             rows = slice(b * block, (b + 1) * block)
             here = jnp.dot(
-                v_turn[second, :, rows], p_buf[h % 2, rows, :], preferred_element_type=jnp.float32
+                v_turn[slot, :, rows], p_buf[h % 2, rows, :], preferred_element_type=jnp.float32
             )
             return here if total is None else total + here
 
@@ -488,7 +489,7 @@
                     following = score_block(h + 1, b, following)
                 weigh_block(h, b, highest)
                 if b % pairs == h:
-                    turn_values(following_c, 1 - second, b)
+                    turn_values(following_c, 1 - slot, b)
                 if b > 0:
                     mixed = value_block(h, b - 1, mixed)
             mixed = value_block(h, BLOCKS - 1, mixed)
@@ -504,15 +505,11 @@
             for copy in y_copies(row):
                 copy.start()
 
-        @pl.when(t == 3)
-        def _():
-            merge(near_first(z, 0), False)
-
-        @pl.when(t == 5)
+        @pl.when(t == 4)
         def _():
             merge(near_first(z, 1), True)
 
-        @pl.when(t == 7)
+        @pl.when(t == 6)
         def _():
             merge(near_first(z, 2), True)
 
@@ -533,6 +530,7 @@
         own.append(partial)
 
     merge(near_first(z, 3), True)
+    merge(z, False)
 
     def from_row(row):
         return (

time: 157 us -> 147 us (0.936)
  Pallas kernels: 152 us -> 142 us
    pallas_call x1, Pallas kernels: 152 us -> 142 us  [plane_call(): pl.pallas_call(plane_kernel, out_shape=jax.ShapeDtypeStruct(fresh.shape,...]
where the time goes in v7:
time: 147 us
  Pallas kernels  142 us (97%)
  local copies, waits for them, and re-layouts  3.13 us (2%)
    pallas_call x1, Pallas kernels, plane_call(): pl.pallas_call(plane_kernel, out_shape=jax.ShapeDtypeStruct(fresh.shape,...  142 us
    unnamed x1, local copies, waits for them, and re-layouts  3.13 us

profile of v7, /device:TPU:2, one launch (start us, length us, event | category | flops | bytes accessed | tf_op | source)
XLA Modules:
  0.0 147.0 jit_solution(12783723558718683447)
XLA Ops:
  0.7 0.5 fusion
  1.2 0.8 pad_maximum_fusion
  2.1 141.8 %shard_map.100 = bf16[256,4096]{1,0:T(8,128)(2,1)} custom-call(s32[1,8]{1,0:T(1,128)} %counts_ref.1, f32[1,4096]{1,0:T(1,128)} %gain_ref.1, f32[256,128]{1,0:T(8,128)} %get-tuple-element.8.cos_ref, f32[256,128]{1,0:T(8,128)} %get-tuple-element.9.sin_ref, bf16[256,4096]{1,0:T(8,128)(2,1)} %fresh_hbm.1, bf16[256,4096]{1,0:T(8,128)(2,1)} %bitcast.13, ...), custom_call_target="tpu_custom_call" | custom-call | flops 8589934592 | bytes 20971520 | tf_op jit(solution)/shard_map/pallas_call | solution.py:681
  143.8 3.1 %copy.13 = bf16[1,256,4096]{2,1,0:T(8,128)(2,1)} copy(bf16[1,256,4096]{2,1,0:T(8,128)(2,1)} %bitcast.8) | data formatting | bytes 4194304
  (2 shorter events, 0.0 us)
